TPU v7x, 256 devices: a whole 4x4x8 slice. The times are simulated.
256 devices in a mesh: ctx: 16 (over z, core), exp: 16 (over x, y).
Axes of the slice: x: 4, y: 4, z: 8, core: 2. Of those that a mesh axis runs over, the one named last changes fastest.
Arguments:
- q_pref: bfloat16 [2048, 128, 576], P('ctx', 'exp'), may hold values from -10 to 10
- kv_pref: bfloat16 [2048, 576], P('ctx'), may hold values from -4 to 4
- dec_q: bfloat16 [256, 128, 576], P('exp', 'ctx'), may hold values from -10 to 10
- dec_kv: bfloat16 [256, 576], P('exp'), may hold values from -4 to 4
- page_req: int32 [16, 16], P('exp'), may hold values from 0 to 127, as said below
- dec_len: int32 [256], P('exp'), may hold values from 1 to 256, as said below
- w_uv: bfloat16 [128, 512, 128], P('ctx'), may hold values from -1 to 1
- w_o: bfloat16 [16384, 7168], P('ctx', 'exp'), may hold values from -0.09375 to 0.09375
- x_dec: bfloat16 [256, 7168], P('exp'), may hold values from -6 to 6
- norm_gain: bfloat16 [7168], replicated, may hold values from 0.5 to 1.5
- router: bfloat16 [7168, 16], replicated, may hold values from -0.0625 to 0.0625
- routes: int32 [256, 8], P('exp'), may hold values from 0 to 15, all different within a row; in each aligned block of 16 rows (0 to 15, 16 to 31, ...) at most 10 rows name the same one
- w_gate: bfloat16 [16, 7168, 2048], P('exp', None, 'ctx'), may hold values from -0.0625 to 0.0625
- w_up: bfloat16 [16, 7168, 2048], P('exp', None, 'ctx'), may hold values from -0.0625 to 0.0625
- w_down: bfloat16 [16, 2048, 7168], P('exp', 'ctx'), may hold values from -0.125 to 0.125
Outputs:
- pref_out: bfloat16 [2048, 128, 512], P('ctx', 'exp')
- decode_out: bfloat16 [256, 7168], P('exp')
Inputs may be any that keep to these rules, and one draw needn't show every extreme that they name: `page_req`: entries of one list differ. Pages i * 8 to (i + 1) * 8 - 1 belong to index i of ctx; a list names at most 2 pages of one index, and every list names exactly 2 pages of some index. `dec_len`: every index of exp holds a row whose length is 256. `routes`: each row names 8 different experts; the rows of one index of exp name one expert at most 10 times.
All inputs are finite; a program needn't handle non-finite values.
Results may differ from a plain program's by a relative error of at most 0.019.
Values may be sent and summed in bfloat16 or wider, within the bound.
A program may use at most 192 MiB of HBM per device.

v0:
```python
import jax
import jax.numpy as jnp
from jax import lax
from jax.sharding import PartitionSpec as P

PAGE = 16
CAPP = 2
CAPE = 10


qk_scale = 192.0 ** (-0.5)
neg_big = -1e30


def body(
    q_pref,
    kv_pref,
    dec_q,
    dec_kv,
    page_req,
    dec_len,
    w_uv,
    w_o,
    x_dec,
    norm_gain,
    router,
    routes,
    w_gate,
    w_up,
    w_down,
):
    tokens, pref_heads, latent = q_pref.shape
    value_width = w_uv.shape[1]
    ctx_index = lax.axis_index("ctx")
    query_count = tokens * pref_heads
    queries = q_pref.reshape(query_count, latent)
    query_pos = ctx_index * tokens + jnp.arange(query_count) // pref_heads
    start_state = (
        jnp.full((query_count,), neg_big, jnp.float32),
        jnp.zeros((query_count,), jnp.float32),
        jnp.zeros((query_count, value_width), jnp.float32),
    )
    carry_state = start_state
    key_piece = lax.all_gather(kv_pref, "ctx", axis=0, tiled=True)
    key_blocks = key_piece.reshape(key_piece.shape[0] // tokens, tokens, latent)

    def key_step(fold_carry, block_item):
        block_offset, key_block = block_item
        running_max, weight_sum, accumulated = fold_carry
        key_pos = block_offset * tokens + jnp.arange(tokens)
        scores = (
            jnp.einsum("qc,kc->qk", queries, key_block, preferred_element_type=jnp.float32)
            * qk_scale
        )
        allowed = key_pos[None, :] <= query_pos[:, None]
        new_max = jnp.maximum(running_max, jnp.max(jnp.where(allowed, scores, neg_big), axis=1))
        weights = jnp.where(allowed, jnp.exp(scores - new_max[:, None]), 0.0)
        rescale = jnp.exp(running_max - new_max)
        weight_sum = weight_sum * rescale + jnp.sum(weights, axis=1)
        accumulated = accumulated * rescale[:, None] + jnp.dot(
            weights.astype(jnp.bfloat16),
            key_block[:, :value_width],
            preferred_element_type=jnp.float32,
        )
        return ((new_max, weight_sum, accumulated), None)

    carry_state, _ = lax.scan(key_step, carry_state, (jnp.arange(key_blocks.shape[0]), key_blocks))
    running_max, weight_sum, accumulated = carry_state
    pref_out = (
        (accumulated / weight_sum[:, None])
        .astype(jnp.bfloat16)
        .reshape(tokens, pref_heads, value_width)
    )
    page_count = tokens // PAGE
    wanted = page_req[0]
    source = wanted // page_count
    earlier = jnp.arange(wanted.shape[0])
    same_source = (source[:, None] == source[None, :]) & (earlier[None, :] < earlier[:, None])
    source_rank = jnp.sum(same_source.astype(jnp.int32), axis=1)
    held_here = source == ctx_index
    slot_pick = (held_here[None, :] & (source_rank[None, :] == jnp.arange(CAPP)[:, None])).astype(
        jnp.bfloat16
    )
    page_pick = ((wanted % page_count)[:, None] == jnp.arange(page_count)[None, :]).astype(
        jnp.bfloat16
    )
    selector = jnp.dot(slot_pick, page_pick, preferred_element_type=jnp.float32).astype(
        jnp.bfloat16
    )
    outgoing = jnp.dot(
        selector, kv_pref.reshape(page_count, PAGE * latent), preferred_element_type=jnp.float32
    ).astype(jnp.bfloat16)
    arrived = lax.all_gather(outgoing, "ctx", axis=0, tiled=True)
    key_cache = arrived[source * CAPP + source_rank].reshape(-1, latent)
    cache_len = key_cache.shape[0]
    scores = (
        jnp.einsum("rhc,kc->rhk", dec_q, key_cache, preferred_element_type=jnp.float32) * qk_scale
    )
    own_score = (
        jnp.einsum("rhc,rc->rh", dec_q, dec_kv, preferred_element_type=jnp.float32) * qk_scale
    )
    allowed = jnp.arange(cache_len)[None, None, :] < dec_len[:, None, None]
    row_max = jnp.maximum(jnp.max(jnp.where(allowed, scores, neg_big), axis=2), own_score)
    weights = jnp.where(allowed, jnp.exp(scores - row_max[..., None]), 0.0)
    own_weight = jnp.exp(own_score - row_max)
    total_weight = jnp.sum(weights, axis=2) + own_weight
    own_round = lax.optimization_barrier(own_weight.astype(jnp.bfloat16)).astype(jnp.float32)
    mixed_sum = jnp.einsum(
        "rhk,kc->rhc",
        weights.astype(jnp.bfloat16),
        key_cache[:, :value_width],
        preferred_element_type=jnp.float32,
    )
    mixed_sum = mixed_sum + own_round[..., None] * dec_kv[:, None, :value_width].astype(jnp.float32)
    dec_lat = (mixed_sum / total_weight[..., None]).astype(jnp.bfloat16)
    head_vals = jnp.einsum(
        "rhc,hcv->rhv", dec_lat, w_uv, preferred_element_type=jnp.float32
    ).astype(jnp.bfloat16)
    flat_vals = head_vals.reshape(head_vals.shape[0], -1)
    partial_value = jnp.dot(
        lax.all_gather(flat_vals, "exp", axis=0, tiled=True),
        w_o,
        preferred_element_type=jnp.float32,
    )
    summed = lax.psum(partial_value.astype(jnp.bfloat16), "ctx").astype(jnp.float32)
    head_out = lax.all_to_all(
        summed.astype(jnp.bfloat16), "exp", split_axis=0, concat_axis=1, tiled=True
    ).astype(summed.dtype)
    residual = x_dec.astype(jnp.float32) + head_out
    normed = (
        residual
        * lax.rsqrt(jnp.mean(residual * residual, axis=-1, keepdims=True) + 1e-06)
        * norm_gain.astype(jnp.float32)
    ).astype(jnp.bfloat16)
    affinity = jax.nn.sigmoid(jnp.dot(normed, router, preferred_element_type=jnp.float32))
    expert_count = router.shape[1]
    chosen = routes[:, :, None] == jnp.arange(expert_count)[None, None, :]
    picked = jnp.sum(jnp.where(chosen, affinity[:, None, :], 0.0), axis=2)
    gate_share = 2.5 * picked / jnp.sum(picked, axis=1, keepdims=True)
    per_expert = jnp.sum(jnp.where(chosen, gate_share[:, :, None], 0.0), axis=1)
    routed = jnp.any(chosen, axis=1)
    position = jnp.cumsum(routed.astype(jnp.int32), axis=0) - 1
    dispatch = routed.T[:, None, :] & (position.T[:, None, :] == jnp.arange(CAPE)[None, :, None])
    packed = jnp.einsum(
        "ecr,rd->ecd", dispatch.astype(jnp.bfloat16), normed, preferred_element_type=jnp.float32
    ).astype(jnp.bfloat16)
    local_experts = w_gate.shape[0]
    outgoing_rows = packed.reshape(
        expert_count // local_experts, local_experts, CAPE, packed.shape[2]
    )
    arrived_rows = lax.all_to_all(outgoing_rows, "exp", split_axis=0, concat_axis=0, tiled=True)
    gate_val = jnp.einsum(
        "sjcd,jdf->sjcf", arrived_rows, w_gate, preferred_element_type=jnp.float32
    )
    up_val = jnp.einsum("sjcd,jdf->sjcf", arrived_rows, w_up, preferred_element_type=jnp.float32)
    hidden = (jax.nn.silu(gate_val) * up_val).astype(jnp.bfloat16)
    partial_out = jnp.einsum("sjcf,jfd->sjcd", hidden, w_down, preferred_element_type=jnp.float32)
    share_weight = dispatch.astype(jnp.float32) * per_expert.T[:, None, :]
    summed_out = lax.psum(partial_out.astype(jnp.bfloat16), "ctx").astype(jnp.float32)
    returned = (
        lax.all_to_all(
            summed_out.astype(jnp.bfloat16), "exp", split_axis=0, concat_axis=0, tiled=True
        )
        .astype(summed_out.dtype)
        .reshape(expert_count, CAPE, -1)
    )
    routed_sum = jnp.einsum("ecr,ecd->rd", share_weight, returned, precision=lax.Precision.HIGHEST)
    decode_out = (residual + routed_sum).astype(jnp.bfloat16)
    return (pref_out, decode_out)


def solution(mesh):
    placed = (
        P("ctx", "exp", None),
        P("ctx", None),
        P("exp", "ctx", None),
        P("exp", None),
        P("exp", None),
        P("exp"),
        P("ctx", None, None),
        P("ctx", "exp"),
        P("exp", None),
        P(),
        P(),
        P("exp", None),
        P("exp", None, "ctx"),
        P("exp", None, "ctx"),
        P("exp", "ctx", None),
    )
    return jax.shard_map(
        body,
        mesh=mesh,
        in_specs=placed,
        out_specs=(P("ctx", "exp", None), P("exp", None)),
        check_vma=False,
    )
```

profile of v0, /device:TPU:1, one launch (start us, length us, event | category | flops | bytes accessed | tf_op | source)
XLA Modules:
  0.0 540.2 jit_solution(1184142004912927604)
XLA Ops:
  11.1 22.9 %all-gather = bf16[16,2,9216]{2,1,0:T(2,128)(2,1)S(1)} all-gather(bf16[1,2,9216]{2,1,0:T(2,128)(2,1)S(1)} %fusion.19), channel_id=1, replica_groups=mesh['ctx'=16,'exp'=16] {'ctx'}, dimensions={0}, use_global_device_ids=true | all-gather | bytes 626688 | tf_op jit(solution)/shard_map/all_gather | solution.py:93
  38.0 19.1 %all_gather.11 = bf16[256,1024]{1,0:T(8,128)(2,1)S(1)} all-gather(bf16[16,1024]{1,0:T(8,128)(2,1)S(1)} %bitcast.189), channel_id=1, replica_groups=mesh['ctx'=16,'exp'=16] {'exp'}, dimensions={0}, use_global_device_ids=true | all-gather | bytes 557056 | tf_op jit(solution)/shard_map/all_gather | solution.py:121
  58.7 109.1 %all-reduce.3.cloned.1.call-done = bf16[16,16,448]{2,1,0:T(8,128)(2,1)} async-done(((bf16[16,16,448]{2,1,0:T(8,128)(2,1)}), bf16[16,16,448]{2,1,0:T(8,128)(2,1)}) %all-reduce.3.cloned.1.call-update) | async-done | bytes 229392 | tf_op jit(solution)/shard_map/psum | solution.py:125
  167.7 6.5 %all-to-all-start = ((bf16[16,16,448]{2,1,0:T(8,128)(2,1)}), bf16[16,16,448]{2,1,0:T(8,128)(2,1)S(1)}, u32[]{:S(2)}, u32[]{:S(2)}) async-start(bf16[16,16,448]{2,1,0:T(8,128)(2,1)} %all-reduce.3.cloned.1.call-done), calls=%async_computation | async-start | bytes 524288 | tf_op jit(solution)/shard_map/all_to_all | solution.py:126
  174.3 7.4 %all-to-all-done = bf16[16,16,448]{2,1,0:T(8,128)(2,1)S(1)} async-done(((bf16[16,16,448]{2,1,0:T(8,128)(2,1)}), bf16[16,16,448]{2,1,0:T(8,128)(2,1)S(1)}, u32[]{:S(2)}, u32[]{:S(2)}) %all-to-all-start) | async-done | bytes 229408 | tf_op jit(solution)/shard_map/all_to_all | solution.py:126
  184.9 46.6 %all_to_all.23 = bf16[16,1,10,7168]{3,2,1,0:T(8,128)(2,1)S(1)} all-to-all(bf16[16,1,10,7168]{3,2,1,0:T(8,128)(2,1)S(1)} %copy.58), channel_id=1, replica_groups=mesh['ctx'=16,'exp'=16] {'exp'}, dimensions={0} | all-to-all | bytes 4587520 | tf_op jit(solution)/shard_map/all_to_all | solution.py:151
  234.8 6.2 %fusion.21 = bf16[16,1,10,7168]{3,0,2,1:T(8,128)(2,1)} fusion(bf16[1,128,7168]{2,1,0:T(8,128)(2,1)S(1)} %copy-done, bf16[1,7168,128]{2,1,0:T(8,128)(2,1)} %param.30, bf16[16,1,10,7168]{3,2,1,0:T(8,128)(2,1)} %copy-done.1, f32[16,1,10,128]{3,0,2,1:T(8,128)S(1)} %fusion.39), kind=kOutput, calls=%fused_computation.36 | convolution fusion | flops 588472320 | bytes 8339456 | tf_op jit(solution)/shard_map/sjcf,jfd->sjcd/dot_general | solution.py:157
  245.3 110.4 %all-reduce.5.cloned.1.call-done = bf16[16,1,10,7168]{3,0,2,1:T(8,128)(2,1)} async-done(((bf16[16,1,10,7168]{3,0,2,1:T(8,128)(2,1)}), bf16[16,1,10,7168]{3,0,2,1:T(8,128)(2,1)}) %all-reduce.5.cloned.1.call-update) | async-done | bytes 2293776 | tf_op jit(solution)/shard_map/psum | solution.py:159
  355.7 4.8 copy.60
  360.6 6.6 %all-to-all-start.2 = ((bf16[16,1,10,7168]{3,2,1,0:T(8,128)(2,1)}), bf16[16,1,10,7168]{3,2,1,0:T(8,128)(2,1)}, u32[]{:S(2)}, u32[]{:S(2)}) async-start(bf16[16,1,10,7168]{3,2,1,0:T(8,128)(2,1)} %copy.60), calls=%async_computation.2 | async-start | bytes 7340032 | tf_op jit(solution)/shard_map/all_to_all | solution.py:161
  367.2 33.0 %all-gather.3.cloned.1.call-done = bf16[2048,576]{0,1:T(8,128)(2,1)} async-done(((bf16[128,576]{0,1:T(8,128)(2,1)}), bf16[2048,576]{0,1:T(8,128)(2,1)}) %all-gather.3.cloned.1.call-update) | async-done | bytes 2359312 | tf_op jit(solution)/shard_map/all_gather | solution.py:44
  400.2 4.3 copy.48
  404.5 120.8 %while.15 = (s32[]{:T(128)}, f32[1024]{0:T(1024)S(1)}, f32[1024]{0:T(1024)S(1)}, f32[1024,512]{1,0:T(8,128)}, s32[16]{0:T(128)S(1)}, /*index=5*/bf16[16,128,576]...) while((s32[]{:T(128)}, f32[1024]{0:T(1024)S(1)}, ...), condition=%wide.region_3.4_spmd.clone, body=%wide.region_0.3_spmd.clone.sunk | while | flops 288372864 | bytes 7604381 | solution.py:67
  422.4 3.5 fusion.153
  430.0 3.5 fusion.153
  445.3 3.5 fusion.153
  453.0 3.5 fusion.153
  468.3 3.5 fusion.153
  475.9 3.5 fusion.153
  491.2 3.5 fusion.153
  498.9 3.5 fusion.153
  514.2 3.5 fusion.153
  521.8 3.5 fusion.153
  528.1 5.6 %fusion.23 = bf16[16,7168]{1,0:T(8,128)(2,1)} fusion(bf16[16,1,10,7168]{3,2,1,0:T(8,128)(2,1)} %all-to-all-done.2, f32[16,7168]{1,0:T(8,128)S(1)} %reshape.255, bf16[16,7168]{1,0:T(8,128)(2,1)S(1)} %copy-done.3, f32[16,16]{0,1:T(8,128)S(1)} %bitcast.193, s32[16,16]{0,1:T(8,128)S(1)} %add_bitcast_fusion, pred[16,16]{0,1:T(8,128)(4,1)S(1)} %bitcast.191), kind=kOutput, calls=%fused_computation.39 | convolution fusion | flops 220667392 | bytes 3213568 | tf_op jit(solution)/shard_map/ecr,ecd->rd/dot_general | solution.py:167
  (228 shorter events, 98.9 us)
Async XLA Ops:
  7.2 227.6 %copy-start = (bf16[1,128,7168]{2,1,0:T(8,128)(2,1)S(1)}, bf16[1,128,7168]{2,1,0:T(8,128)(2,1)}, u32[]{:S(2)}) copy-start(bf16[1,128,7168]{2,1,0:T(8,128)(2,1)} %param.31) | copy-start | bytes 5505028
  7.2 160.5 %all-reduce.3.cloned.1.call-start = ((), (), s32[]{:S(2)}) async-start(), calls=%async_computation.4 | async-start | bytes 524288 | tf_op jit(solution)/shard_map/psum | solution.py:125
  34.1 1.3 copy-start.8
  34.1 1.4 copy-start.6
  34.1 1.4 copy-start.10
  35.3 21.7 %copy-start.2 = (bf16[1024,448]{0,1:T(8,128)(2,1)S(1)}, bf16[1024,448]{0,1:T(8,128)(2,1)}, u32[]{:S(2)}) copy-start(bf16[1024,448]{0,1:T(8,128)(2,1)} %param.24) | copy-start | bytes 2752516
  36.3 22.1 %copy-start.5 = (bf16[7168]{0:T(1024)(128)(2,1)S(1)}, bf16[7168]{0:T(1024)(128)(2,1)}, u32[]{:S(2)}) copy-start(bf16[7168]{0:T(1024)(128)(2,1)} %param.26) | copy-start | bytes 43012
  36.3 22.1 %copy-start.7 = (s32[16,8]{0,1:T(8,128)S(1)}, s32[16,8]{0,1:T(8,128)}, u32[]{:S(2)}) copy-start(s32[16,8]{0,1:T(8,128)} %param.28) | copy-start | bytes 1540
  57.5 124.8 %copy-start.3 = (bf16[16,7168]{1,0:T(8,128)(2,1)S(1)}, bf16[16,7168]{1,0:T(8,128)(2,1)}, u32[]{:S(2)}) copy-start(bf16[16,7168]{1,0:T(8,128)(2,1)} %param.25) | copy-start | bytes 688132
  167.7 14.0 %all-to-all-start = ((bf16[16,16,448]{2,1,0:T(8,128)(2,1)}), bf16[16,16,448]{2,1,0:T(8,128)(2,1)S(1)}, u32[]{:S(2)}, u32[]{:S(2)}) async-start(bf16[16,16,448]{2,1,0:T(8,128)(2,1)} %all-reduce.3.cloned.1.call-done), calls=%async_computation | async-start | bytes 524288 | tf_op jit(solution)/shard_map/all_to_all | solution.py:126
  174.2 181.5 %all-reduce.5.cloned.1.call-start = ((), (), s32[]{:S(2)}) async-start(), calls=%async_computation.5 | async-start | bytes 4587520 | tf_op jit(solution)/shard_map/psum | solution.py:159
  184.9 48.4 %copy-start.9 = (bf16[1,7168,128]{2,1,0:T(8,128)(2,1)S(1)}, bf16[1,7168,128]{2,1,0:T(8,128)(2,1)}, u32[]{:S(2)}) copy-start(bf16[1,7168,128]{2,1,0:T(8,128)(2,1)} %param.29) | copy-start | bytes 5505028
  231.4 1.8 copy-start.1
  241.0 3.7 copy-start.4
  241.0 159.2 %all-gather.3.cloned.1.call-start = ((), (), s32[]{:S(2)}) async-start(), calls=%async_computation.3 | async-start | bytes 2506752 | tf_op jit(solution)/shard_map/all_gather | solution.py:44
  360.6 167.6 %all-to-all-start.2 = ((bf16[16,1,10,7168]{3,2,1,0:T(8,128)(2,1)}), bf16[16,1,10,7168]{3,2,1,0:T(8,128)(2,1)}, u32[]{:S(2)}, u32[]{:S(2)}) async-start(bf16[16,1,10,7168]{3,2,1,0:T(8,128)(2,1)} %copy.60), calls=%async_computation.2 | async-start | bytes 7340032 | tf_op jit(solution)/shard_map/all_to_all | solution.py:161
Sparse Core Ops, SparseCore 0:
  58.5 109.1 all-reduce.2
  241.1 114.5 all-reduce.4
  357.6 42.5 all-gather.2
where the time goes:
time: 542 us; the launch traced here: 540 us
  waiting for transfers between devices  260 us (48%)
  matrix products  102 us (19%)
  blocking collectives  88.6 us (16%)
  local copies, waits for them, and re-layouts  43.1 us (8%)
  between operations  14.1 us (3%)
  starting transfers between devices  13.4 us (2%)
  loops' own time  9.68 us (2%)
  other arithmetic  9 us (2%)
    psum x1, waiting for transfers between devices, body(): lax.psum(partial_out.astype(jnp.bfloat16), 'ctx').astype(jnp.float32)  110 us
    psum x1, waiting for transfers between devices, body(): lax.psum(partial_value.astype(jnp.bfloat16), 'ctx').astype(jnp.float32)  109 us
    dot_general x16, matrix products, key_step(): jnp.dot(weights.astype(jnp.bfloat16), key_block[:, :value_width], preferr...  54.6 us
    all_to_all x1, blocking collectives, body(): lax.all_to_all(outgoing_rows, 'exp', split_axis=0, concat_axis=0, tiled=T...  46.6 us
    all_gather x1, waiting for transfers between devices, body(): key_piece = lax.all_gather(kv_pref, 'ctx', axis=0, tiled=True)  33 us
    dot_general x16, matrix products, key_step(): jnp.einsum('qc,kc->qk', queries, key_block, preferred_element_type=jnp.fl...  30.2 us
    all_gather x1, blocking collectives, body(): arrived = lax.all_gather(outgoing, 'ctx', axis=0, tiled=True)  22.9 us
    all_gather x1, blocking collectives, body(): lax.all_gather(flat_vals, 'exp', axis=0, tiled=True)  19.1 us
  transfers between devices with their start and end apart: 5, of which 4 were waited for; matrix products, arithmetic and copies ran while one was open for 23% of the time, Pallas kernels for 0%

commit v1 on v0

v1 whole, which is shorter than its diff:
```python
import functools

import jax
import jax.numpy as jnp
from jax import lax
from jax.experimental import pallas as pl
from jax.experimental.pallas import tpu as pltpu
from jax.sharding import PartitionSpec as P

D = 7168
HALF = D // 2
KVL = 512
LAT = 576
HEADS_DEV = 8
VD = 128
FF = 128
TOK = 128
PAGE = 16
GROUP = 16
COLS = 448
EXT = 128
WIDE = HALF + EXT
PIECE = 512

qk_scale = 192.0 ** (-0.5)
neg_big = -1e30
MESH = pl.DeviceIdType.MESH
VMEM = pltpu.VMEM
ANY = pl.ANY
LIMIT = 56 * 1024 * 1024


class Place:
    def __init__(self):
        self.c = lax.axis_index("ctx")
        self.e = lax.axis_index("exp")
        self.z, self.k = self.c // 2, self.c % 2
        x, y = self.e // 4, self.e % 4
        self.a = x + self.k * (y - x)
        self.b = y + self.k * (x - y)

    def exp_of(self, a, b):
        return (a + self.k * (b - a)) * 4 + b + self.k * (a - b)

    def plane(self, a, b):
        return (self.c, self.exp_of(a % 4, b % 4))

    def sibling(self):
        return (self.c + 1 - 2 * self.k, self.e)

    def along_z(self, step):
        return (((self.z + step) % 8) * 2 + self.k, self.e)


def greet(devices):
    barrier = pltpu.get_barrier_semaphore()
    for device in devices:
        pl.semaphore_signal(barrier, inc=1, device_id=device, device_id_type=MESH)
    pl.semaphore_wait(barrier, len(devices))


class Wires:
    def __init__(self, send_sem, recv_sem):
        self.send_sem, self.recv_sem = send_sem, recv_sem
        self.count = 0
        self.open = []

    def copy(self, src, dst, device):
        i = self.count
        self.count += 1
        made = pltpu.make_async_remote_copy(
            src_ref=src,
            dst_ref=dst,
            send_sem=self.send_sem.at[i],
            recv_sem=self.recv_sem.at[i],
            device_id=device,
            device_id_type=MESH,
        )
        made.start()
        self.open.append(made)
        return made

    def drain(self):
        for made in self.open:
            made.wait_send()
        self.open = []


def plane_gather(place, wires, buf, first):
    a, b = place.a, place.b
    lo, hi = pl.ds(0, first), pl.ds(first, buf.shape[2] - first)

    def slot(i, j):
        return (j % 4) * 4 + i % 4

    def both(ref, right, left):
        return wires.copy(ref, ref, right), wires.copy(ref, ref, left)

    def relay(i, j, i2, j2, right, left, got):
        got[0].wait_recv()
        one = buf.at[slot(i, j), :, lo]
        first_half = wires.copy(one, one, right)
        got[1].wait_recv()
        two = buf.at[slot(i2, j2), :, hi]
        return first_half, wires.copy(two, two, left)

    a_right, a_left = place.plane(a + 1, b), place.plane(a - 1, b)
    b_right, b_left = place.plane(a, b + 1), place.plane(a, b - 1)
    mine = buf.at[slot(a, b)]
    near = both(mine, a_right, a_left)
    columns = [(0, both(mine, b_right, b_left))]
    far = relay(a - 1, b, a + 1, b, a_right, a_left, near)
    for step in (-1, 1):
        ref = buf.at[slot(a + step, b)]
        columns.append((step, both(ref, b_right, b_left)))
    halves = []
    for step, got in columns[:2]:
        halves.append(relay(a + step, b - 1, a + step, b + 1, b_right, b_left, got))
    far[0].wait_recv()
    far[1].wait_recv()
    ref = buf.at[slot(a + 2, b)]
    columns.append((2, both(ref, b_right, b_left)))
    for step, got in columns[2:]:
        halves.append(relay(a + step, b - 1, a + step, b + 1, b_right, b_left, got))

    def finish():
        for one, two in halves:
            one.wait_recv()
            two.wait_recv()

    return finish


GATHER_COPIES = 20


def ring_sum(wires, right, left, piece, rx1r, rx1l, t_r, t_l, rx2r, rx2l, first):
    far = piece(2)
    lo, hi = pl.ds(0, first), pl.ds(first, far.shape[-1] - first)
    one = wires.copy(far.at[..., lo], rx1r, right)
    two = wires.copy(far.at[..., hi], rx1l, left)
    one.wait_recv()
    near = piece(1)
    t_r[..., hi] = near[..., hi]
    t_r[..., lo] = (near[..., lo].astype(jnp.float32) + rx1r[...].astype(jnp.float32)).astype(
        jnp.bfloat16
    )
    three = wires.copy(t_r, rx2r, right)
    two.wait_recv()
    near = piece(-1)
    t_l[..., lo] = near[..., lo]
    t_l[..., hi] = (near[..., hi].astype(jnp.float32) + rx1l[...].astype(jnp.float32)).astype(
        jnp.bfloat16
    )
    four = wires.copy(t_l, rx2l, left)
    three.wait_recv()
    four.wait_recv()
    return (
        piece(0)[...].astype(jnp.float32)
        + rx2r[...].astype(jnp.float32)
        + rx2l[...].astype(jnp.float32)
    )


def keys_kernel(kv, gate, up, down, keys, s_gate, s_up, s_down, send, recv, here):
    place = Place()
    z, k = place.z, place.k
    sibling, right, left = place.sibling(), place.along_z(1), place.along_z(-1)
    greet([sibling, right, left])
    wires = Wires(send, recv)

    def slot(step):
        return ((z + step) % 8) * 2 + k

    mine = keys.at[slot(0)]
    to_r = wires.copy(kv, mine, right)
    to_l = wires.copy(kv, mine, left)
    from_sibling = [wires.copy(kv, mine, sibling)]
    local = pltpu.make_async_copy(kv, mine, here)
    local.start()
    other = pl.ds((1 - k) * HALF, HALF)
    swaps = [
        wires.copy(gate.at[0, other, :], s_gate, sibling),
        wires.copy(up.at[0, other, :], s_up, sibling),
        wires.copy(down.at[0, :, other], s_down, sibling),
    ]
    for hop in (1, 2, 3):
        to_r.wait_recv()
        ref = keys.at[slot(-hop)]
        part = ref if hop < 3 else keys.at[slot(-hop), pl.ds(0, TOK // 2), :]
        to_r = wires.copy(part, part, right)
        from_sibling.append(wires.copy(ref, ref, sibling))
        to_l.wait_recv()
        ref = keys.at[slot(hop)]
        part = ref if hop < 3 else keys.at[slot(hop), pl.ds(TOK // 2, TOK // 2), :]
        to_l = wires.copy(part, part, left)
        from_sibling.append(wires.copy(ref, ref, sibling))
    to_r.wait_recv()
    to_l.wait_recv()
    ref = keys.at[slot(4)]
    from_sibling.append(wires.copy(ref, ref, sibling))
    for made in from_sibling + swaps:
        made.wait_recv()
    local.wait()
    wires.drain()


def gather_keys(kv, w_gate, w_up, w_down):
    copies = 2 + 1 + 3 + 3 * 4 + 1
    return pl.pallas_call(
        keys_kernel,
        out_shape=(
            jax.ShapeDtypeStruct((16, TOK, LAT), jnp.bfloat16),
            jax.ShapeDtypeStruct((HALF, FF), jnp.bfloat16),
            jax.ShapeDtypeStruct((HALF, FF), jnp.bfloat16),
            jax.ShapeDtypeStruct((FF, HALF), jnp.bfloat16),
        ),
        in_specs=[pl.BlockSpec(memory_space=ANY)] * 4,
        out_specs=[pl.BlockSpec(memory_space=ANY)] * 4,
        scratch_shapes=[
            pltpu.SemaphoreType.DMA((copies,)),
            pltpu.SemaphoreType.DMA((copies,)),
            pltpu.SemaphoreType.DMA,
        ],
        compiler_params=pltpu.CompilerParams(collective_id=1, has_side_effects=True),
    )(kv, w_gate, w_up, w_down)


def prefill_kernel(q, keys, out):
    rows = q.shape[0] * HEADS_DEV
    c = lax.axis_index("ctx")
    queries = q[...].reshape(rows, LAT)
    scores = lax.dot_general(
        queries, keys[...], (((1,), (1,)), ((), ())), preferred_element_type=jnp.float32
    )
    first = c * TOK + pl.program_id(0) * q.shape[0]
    token = first + lax.broadcasted_iota(jnp.int32, (rows, 1), 0) // HEADS_DEV
    key = lax.broadcasted_iota(jnp.int32, scores.shape, 1)
    scores = jnp.where(key <= token, scores, neg_big)
    top = jnp.max(scores, axis=1, keepdims=True)
    weights = jnp.exp((scores - top) * qk_scale)
    total = jnp.sum(weights, axis=1, keepdims=True)
    mixed = jnp.dot(
        weights.astype(jnp.bfloat16), keys[:, :KVL], preferred_element_type=jnp.float32
    )
    out[...] = (mixed / total).astype(jnp.bfloat16).reshape(out.shape)


def prefill(q, keys):
    tile = 32
    return pl.pallas_call(
        prefill_kernel,
        grid=(q.shape[0] // tile,),
        out_shape=jax.ShapeDtypeStruct((q.shape[0], HEADS_DEV, KVL), jnp.bfloat16),
        in_specs=[
            pl.BlockSpec((tile, HEADS_DEV, LAT), lambda i: (i, 0, 0)),
            pl.BlockSpec(keys.shape, lambda i: (0, 0)),
        ],
        out_specs=pl.BlockSpec((tile, HEADS_DEV, KVL), lambda i: (i, 0, 0)),
        compiler_params=pltpu.CompilerParams(vmem_limit_bytes=LIMIT),
    )(q, keys)


def decode_kernel(pages, lengths, q, own, keys, w_uv, vals, cache, sem):
    copies = []
    for i in range(16):
        page = pages[0, i]
        made = pltpu.make_async_copy(keys.at[page], cache.at[i], sem.at[i])
        made.start()
        copies.append(made)
    rows = HEADS_DEV * GROUP
    queries = q[...].reshape(rows, LAT)
    own_all = jnp.broadcast_to(own[...][None], (HEADS_DEV, GROUP, LAT)).reshape(rows, LAT)
    own_all = own_all.astype(jnp.float32)
    own_score = jnp.sum(queries.astype(jnp.float32) * own_all, axis=1, keepdims=True)
    for made in copies:
        made.wait()
    cached = cache[...].reshape(16 * PAGE, LAT)
    scores = lax.dot_general(
        queries, cached, (((1,), (1,)), ((), ())), preferred_element_type=jnp.float32
    )
    row = lax.broadcasted_iota(jnp.int32, (rows, 1), 0) % GROUP
    limit = jnp.zeros((rows, 1), jnp.int32)
    for i in range(GROUP):
        limit = jnp.where(row == i, lengths[i], limit)
    allowed = lax.broadcasted_iota(jnp.int32, scores.shape, 1) < limit
    scores = jnp.where(allowed, scores, neg_big)
    top = jnp.maximum(jnp.max(scores, axis=1, keepdims=True), own_score)
    weights = jnp.where(allowed, jnp.exp((scores - top) * qk_scale), 0.0)
    own_weight = jnp.exp((own_score - top) * qk_scale)
    total = jnp.sum(weights, axis=1, keepdims=True) + own_weight
    mixed = jnp.dot(
        weights.astype(jnp.bfloat16), cached[:, :KVL], preferred_element_type=jnp.float32
    )
    mixed = mixed + own_weight.astype(jnp.bfloat16).astype(jnp.float32) * own_all[:, :KVL]
    latent = (mixed / total).astype(jnp.bfloat16)
    for h in range(HEADS_DEV):
        part = jnp.dot(
            latent[h * GROUP : (h + 1) * GROUP], w_uv[h], preferred_element_type=jnp.float32
        )
        vals[:, h * VD : (h + 1) * VD] = part.astype(jnp.bfloat16)


def decode_attention(pages, lengths, q, own, keys, w_uv):
    vmem = pl.BlockSpec(memory_space=VMEM)
    smem = pl.BlockSpec(memory_space=pltpu.SMEM)
    return pl.pallas_call(
        decode_kernel,
        out_shape=jax.ShapeDtypeStruct((GROUP, HEADS_DEV * VD), jnp.bfloat16),
        in_specs=[smem, smem, vmem, vmem, pl.BlockSpec(memory_space=ANY), vmem],
        out_specs=vmem,
        scratch_shapes=[
            VMEM((16, PAGE, LAT), jnp.bfloat16),
            pltpu.SemaphoreType.DMA((16,)),
        ],
        compiler_params=pltpu.CompilerParams(vmem_limit_bytes=LIMIT),
    )(pages, lengths, q, own, keys, w_uv)


def project_kernel(
    vals, w_o, out, rows, part, rx_sib, red, rx_z, groups, arrived, send, recv, send2, recv2
):
    place = Place()
    z, k, a, b, c, e = place.z, place.k, place.a, place.b, place.c, place.e
    sibling = place.sibling()
    partners = [sibling] + [place.along_z(d) for d in range(1, 8)]
    for i in range(1, 16):
        other = (e + i) % 16
        partners.append((2 * z, other))
        partners.append((2 * z + 1, other))
    greet(partners)
    wires = Wires(send, recv)
    rows[b * 4 + a] = vals[...]
    finish = plane_gather(place, wires, rows, rows.shape[2] // 2)
    finish()
    product = jnp.dot(
        rows[...].reshape(256, rows.shape[2]), w_o[...], preferred_element_type=jnp.float32
    )
    for s in range(16):
        part[place.exp_of(s % 4, s // 4)] = product[s * 16 : s * 16 + 16].astype(jnp.bfloat16)
    swap = wires.copy(part.at[pl.ds((1 - k) * 8, 8)], rx_sib, sibling)
    swap.wait_recv()
    red[...] = (
        part[pl.ds(k * 8, 8)].astype(jnp.float32) + rx_sib[...].astype(jnp.float32)
    ).astype(jnp.bfloat16)
    spread = []
    for d in range(1, 8):
        spread.append(wires.copy(red.at[(z + d) % 8], rx_z.at[d - 1], place.along_z(d)))
    total = red[z].astype(jnp.float32)
    for d in range(1, 8):
        spread[d - 1].wait_recv()
        total = total + rx_z[d - 1].astype(jnp.float32)
    groups[z] = total.astype(jnp.bfloat16)
    shared = []
    for d in range(1, 8):
        shared.append(wires.copy(groups.at[z], groups.at[z], place.along_z(d)))

    def hand_over(t, core):
        return pltpu.make_async_remote_copy(
            src_ref=groups.at[t],
            dst_ref=arrived.at[e],
            send_sem=send2.at[t, core],
            recv_sem=recv2.at[e],
            device_id=(2 * z + core, 8 * k + t),
            device_id_type=MESH,
        )

    for d in range(8):
        t = (z - d) % 8
        if d > 0:
            shared[d - 1].wait_recv()
        for core in (0, 1):
            itself = (core == k) & (8 * k + t == e)

            @pl.when(jnp.logical_not(itself))
            def _():
                hand_over(t, core).start()

            @pl.when(itself)
            def _():
                arrived[e] = groups[t]

    for s in range(16):
        itself = (e == s) & (e // 8 == k)

        @pl.when(jnp.logical_not(itself))
        def _():
            pltpu.make_async_remote_copy(
                src_ref=groups.at[0],
                dst_ref=arrived.at[s],
                send_sem=send2.at[0, 0],
                recv_sem=recv2.at[s],
                device_id=sibling,
                device_id_type=MESH,
            ).wait_recv()

    out[...] = arrived[...]
    for t in range(8):
        for core in (0, 1):
            itself = (core == k) & (8 * k + t == e)

            @pl.when(jnp.logical_not(itself))
            def _():
                hand_over(t, core).wait_send()

    wires.drain()


def project(vals, w_o):
    vmem = pl.BlockSpec(memory_space=VMEM)
    width = HEADS_DEV * VD
    copies = GATHER_COPIES + 1 + 14
    return pl.pallas_call(
        project_kernel,
        out_shape=jax.ShapeDtypeStruct((16, GROUP, COLS), jnp.bfloat16),
        in_specs=[vmem, vmem],
        out_specs=vmem,
        scratch_shapes=[
            VMEM((16, GROUP, width), jnp.bfloat16),
            VMEM((16, GROUP, COLS), jnp.bfloat16),
            VMEM((8, GROUP, COLS), jnp.bfloat16),
            VMEM((8, GROUP, COLS), jnp.bfloat16),
            VMEM((7, GROUP, COLS), jnp.bfloat16),
            VMEM((8, GROUP, COLS), jnp.bfloat16),
            VMEM((16, GROUP, COLS), jnp.bfloat16),
            pltpu.SemaphoreType.DMA((copies,)),
            pltpu.SemaphoreType.DMA((copies,)),
            pltpu.SemaphoreType.DMA((8, 2)),
            pltpu.SemaphoreType.DMA((16,)),
        ],
        compiler_params=pltpu.CompilerParams(
            collective_id=2, has_side_effects=True, vmem_limit_bytes=LIMIT
        ),
    )(vals, w_o)


def experts_kernel(
    normed, shares, residual, gate, up, down, s_gate, s_up, s_down,
    out, rows, w_in, w_out, mid, rx_mid, parts,
    b1r, b1l, btr, btl, b2r, b2l, a_in, a1r, a1l, atr, atl, a2r, a2l,
    zsum, rx_z, final, send, recv, z_send, z_recv, f_send, f_recv, load,
):
    place = Place()
    z, k, a, b, c, e = place.z, place.k, place.a, place.b, place.c, place.e
    sibling = place.sibling()
    a_right, a_left = place.plane(a + 1, b), place.plane(a - 1, b)
    b_right, b_left = place.plane(a, b + 1), place.plane(a, b - 1)
    partners = [sibling, a_right, a_left, b_right, b_left]
    partners += [place.along_z(d) for d in range(1, 8)]
    greet(partners)
    wires = Wires(send, recv)
    half = pl.ds(k * HALF, HALF)
    mine = b * 4 + a
    rows[mine, :, 0:HALF] = normed[:, half]
    rows[mine, :, HALF:WIDE] = shares[...]
    loads = []
    for i, (src, dst) in enumerate(
        (
            (gate.at[0, half, :], w_in.at[:, pl.ds(0, FF)]),
            (up.at[0, half, :], w_in.at[:, pl.ds(FF, FF)]),
            (s_gate, w_in.at[:, pl.ds(2 * FF, FF)]),
            (s_up, w_in.at[:, pl.ds(3 * FF, FF)]),
            (down.at[0, :, half], w_out.at[pl.ds(0, FF), :]),
            (s_down, w_out.at[pl.ds(FF, FF), :]),
        )
    ):
        made = pltpu.make_async_copy(src, dst, load.at[i])
        made.start()
        loads.append(made)
    finish = plane_gather(place, wires, rows, HALF // 2)
    for made in loads:
        made.wait()
    finish()
    product = jnp.dot(
        rows[:, :, 0:HALF].reshape(256, HALF), w_in[...], preferred_element_type=jnp.float32
    )
    mid[...] = product.reshape(16, 16, 4 * FF)
    swap = wires.copy(mid, rx_mid, sibling)
    extra = rows[:, :, HALF:WIDE].reshape(256, EXT).astype(jnp.float32)
    lane = lax.broadcasted_iota(jnp.int32, (256, EXT), 1)
    share = jnp.sum(
        jnp.where((lane == e) | (lane == e + 16), extra, 0.0), axis=1, keepdims=True
    )
    swap.wait_recv()
    hidden = []
    for s in range(16):
        t = (s % 4) * 4 + s // 4
        own = mid[s]
        other = rx_mid[t]
        g0 = own[:, 0:FF] + other[:, 2 * FF : 3 * FF]
        u0 = own[:, FF : 2 * FF] + other[:, 3 * FF : 4 * FF]
        g1 = own[:, 2 * FF : 3 * FF] + other[:, 0:FF]
        u1 = own[:, 3 * FF : 4 * FF] + other[:, FF : 2 * FF]
        h0 = (jax.nn.silu(g0) * u0).astype(jnp.bfloat16)
        h1 = (jax.nn.silu(g1) * u1).astype(jnp.bfloat16)
        hidden.append(jnp.concatenate([h0, h1], axis=1))
    hidden = jnp.concatenate(hidden, axis=0)
    produced = jnp.dot(hidden, w_out[...], preferred_element_type=jnp.float32) * share
    parts[...] = produced.astype(jnp.bfloat16).reshape(16, 16, HALF)

    total = ring_sum(
        wires,
        b_right,
        b_left,
        lambda d: parts.at[pl.ds(((b + d) % 4) * 4, 4)],
        b1r, b1l, btr, btl, b2r, b2l, HALF // 2,
    )
    a_in[...] = total.astype(jnp.bfloat16)
    total = ring_sum(
        wires,
        a_right,
        a_left,
        lambda d: a_in.at[(a + d) % 4],
        a1r, a1l, atr, atl, a2r, a2l, HALF // 2,
    )
    for i in range(7):
        zsum[i] = total[:, i * PIECE : (i + 1) * PIECE].astype(jnp.bfloat16)

    def spread(d):
        t = (z + d) % 8
        return t < 7, pltpu.make_async_remote_copy(
            src_ref=zsum.at[t % 7],
            dst_ref=rx_z.at[d - 1],
            send_sem=z_send.at[d - 1],
            recv_sem=z_recv.at[d - 1],
            device_id=place.along_z(d),
            device_id_type=MESH,
        )

    for d in range(1, 8):
        used, made = spread(d)

        @pl.when(used)
        def _():
            made.start()

    def share_final(d):
        return pltpu.make_async_remote_copy(
            src_ref=final.at[k, z % 7],
            dst_ref=final.at[k, z % 7],
            send_sem=f_send.at[d - 1],
            recv_sem=f_recv.at[z],
            device_id=place.along_z(d),
            device_id_type=MESH,
        )

    @pl.when(z < 7)
    def _():
        at = z % 7
        mixed = residual[k * 7 + at] + zsum[at].astype(jnp.float32)
        for d in range(1, 8):
            spread(d)[1].wait_recv()
            mixed = mixed + rx_z[d - 1].astype(jnp.float32)
        final[k, at] = mixed.astype(jnp.bfloat16)
        for d in range(1, 8):
            share_final(d).start()

    passed = []
    for i in range(7):

        @pl.when(z != i)
        def _():
            pltpu.make_async_remote_copy(
                src_ref=final.at[k, i],
                dst_ref=final.at[k, i],
                send_sem=f_send.at[0],
                recv_sem=f_recv.at[i],
                device_id=sibling,
                device_id_type=MESH,
            ).wait_recv()

        passed.append(wires.copy(final.at[k, i], final.at[k, i], sibling))
    for made in passed:
        made.wait_recv()
    for j in range(2):
        for i in range(7):
            start = j * HALF + i * PIECE
            out[:, start : start + PIECE] = final[j, i]
    for d in range(1, 8):
        used, made = spread(d)

        @pl.when(used)
        def _():
            made.wait_send()

        @pl.when(z < 7)
        def _():
            share_final(d).wait_send()

    wires.drain()


def experts(normed, shares, residual, w_gate, w_up, w_down, s_gate, s_up, s_down):
    vmem = pl.BlockSpec(memory_space=VMEM)
    anywhere = pl.BlockSpec(memory_space=ANY)
    copies = GATHER_COPIES + 1 + 8 + 7
    bf16, f32 = jnp.bfloat16, jnp.float32
    half = HALF // 2
    return pl.pallas_call(
        experts_kernel,
        out_shape=jax.ShapeDtypeStruct((GROUP, D), bf16),
        in_specs=[vmem] * 3 + [anywhere] * 6,
        out_specs=vmem,
        scratch_shapes=[
            VMEM((16, GROUP, WIDE), bf16),
            VMEM((HALF, 4 * FF), bf16),
            VMEM((2 * FF, HALF), bf16),
            VMEM((16, GROUP, 4 * FF), f32),
            VMEM((16, GROUP, 4 * FF), f32),
            VMEM((16, GROUP, HALF), bf16),
            VMEM((4, GROUP, half), bf16),
            VMEM((4, GROUP, half), bf16),
            VMEM((4, GROUP, HALF), bf16),
            VMEM((4, GROUP, HALF), bf16),
            VMEM((4, GROUP, HALF), bf16),
            VMEM((4, GROUP, HALF), bf16),
            VMEM((4, GROUP, HALF), bf16),
            VMEM((GROUP, half), bf16),
            VMEM((GROUP, half), bf16),
            VMEM((GROUP, HALF), bf16),
            VMEM((GROUP, HALF), bf16),
            VMEM((GROUP, HALF), bf16),
            VMEM((GROUP, HALF), bf16),
            VMEM((7, GROUP, PIECE), bf16),
            VMEM((7, GROUP, PIECE), bf16),
            VMEM((2, 7, GROUP, PIECE), bf16),
            pltpu.SemaphoreType.DMA((copies,)),
            pltpu.SemaphoreType.DMA((copies,)),
            pltpu.SemaphoreType.DMA((7,)),
            pltpu.SemaphoreType.DMA((7,)),
            pltpu.SemaphoreType.DMA((7,)),
            pltpu.SemaphoreType.DMA((8,)),
            pltpu.SemaphoreType.DMA((6,)),
        ],
        compiler_params=pltpu.CompilerParams(
            collective_id=3, has_side_effects=True, vmem_limit_bytes=LIMIT
        ),
    )(normed, shares, residual, w_gate, w_up, w_down, s_gate, s_up, s_down)


def body(
    q_pref,
    kv_pref,
    dec_q,
    dec_kv,
    page_req,
    dec_len,
    w_uv,
    w_o,
    x_dec,
    norm_gain,
    router,
    routes,
    w_gate,
    w_up,
    w_down,
):
    keys, s_gate, s_up, s_down = gather_keys(kv_pref, w_gate, w_up, w_down)
    pages = keys.reshape(16 * TOK // PAGE, PAGE, LAT)
    head_vals = decode_attention(
        page_req, dec_len, jnp.swapaxes(dec_q, 0, 1), dec_kv, pages, w_uv
    )
    head_out = project(head_vals, w_o)
    head_out = jnp.swapaxes(head_out, 0, 1).reshape(GROUP, D)
    residual = x_dec.astype(jnp.float32) + head_out.astype(jnp.float32)
    normed = (
        residual
        * lax.rsqrt(jnp.mean(residual * residual, axis=-1, keepdims=True) + 1e-06)
        * norm_gain.astype(jnp.float32)
    ).astype(jnp.bfloat16)
    affinity = jax.nn.sigmoid(jnp.dot(normed, router, preferred_element_type=jnp.float32))
    chosen = routes[:, :, None] == jnp.arange(router.shape[1])[None, None, :]
    picked = jnp.sum(jnp.where(chosen, affinity[:, None, :], 0.0), axis=2)
    gate_share = 2.5 * picked / jnp.sum(picked, axis=1, keepdims=True)
    per_expert = jnp.sum(jnp.where(chosen, gate_share[:, :, None], 0.0), axis=1)
    high = per_expert.astype(jnp.bfloat16)
    low = (per_expert - high.astype(jnp.float32)).astype(jnp.bfloat16)
    shares = jnp.concatenate([high, low, jnp.zeros((GROUP, EXT - 32), jnp.bfloat16)], axis=1)
    pieces = jnp.swapaxes(residual.reshape(GROUP, 14, PIECE), 0, 1)
    decode_out = experts(
        normed, shares, pieces, w_gate, w_up, w_down, s_gate, s_up, s_down
    )
    pref_out = prefill(q_pref, keys.reshape(16 * TOK, LAT))
    return (pref_out, decode_out)


def solution(mesh):
    placed = (
        P("ctx", "exp", None),
        P("ctx", None),
        P("exp", "ctx", None),
        P("exp", None),
        P("exp", None),
        P("exp"),
        P("ctx", None, None),
        P("ctx", "exp"),
        P("exp", None),
        P(),
        P(),
        P("exp", None),
        P("exp", None, "ctx"),
        P("exp", None, "ctx"),
        P("exp", "ctx", None),
    )
    return jax.shard_map(
        body,
        mesh=mesh,
        in_specs=placed,
        out_specs=(P("ctx", "exp", None), P("exp", None)),
        check_vma=False,
    )
```

time: 542 us -> 155 us (0.29)
  waiting for transfers between devices: 260 us -> 0 us
  Pallas kernels: 0 us -> 143 us
  matrix products: 102 us -> 0.2 us
  blocking collectives: 88.6 us -> 0 us
  local copies, waits for them, and re-layouts: 43.1 us -> 7.98 us
  starting transfers between devices: 13.4 us -> 0 us
  between operations: 14.1 us -> 0.82 us
  loops' own time: 9.68 us -> 0 us
  other arithmetic: 9 us -> 2.5 us
    psum x2 -> x0, waiting for transfers between devices: 219 us -> none  [the longest x1 110 us: body(): lax.psum(partial_out.astype(jnp.bfloat16), 'ctx').astype(jnp.float32)]
    pallas_call x0 -> x5, Pallas kernels: none -> 143 us  [the longest x1 62.9 us: experts(): pl.pallas_call(experts_kernel, out_shape=jax.ShapeDtypeStruct((GROUP, D),...]
    dot_general x41 -> x0, matrix products: 102 us -> none  [the longest x16 54.6 us: key_step(): jnp.dot(weights.astype(jnp.bfloat16), key_block[:, :value_width], preferr...]
    all_to_all x1 -> x0, blocking collectives: 46.6 us -> none  [body(): lax.all_to_all(outgoing_rows, 'exp', split_axis=0, concat_axis=0, tiled=T...]
    all_gather x2 -> x0, blocking collectives: 42 us -> none  [the longest x1 22.9 us: body(): arrived = lax.all_gather(outgoing, 'ctx', axis=0, tiled=True)]
    all_gather x1 -> x0, waiting for transfers between devices: 33 us -> none  [body(): key_piece = lax.all_gather(kv_pref, 'ctx', axis=0, tiled=True)]
    squeeze x16 -> x0, local copies, waits for them, and re-layouts: 15 us -> none  [body(): lax.scan(key_step, carry_state, (jnp.arange(key_blocks.shape[0]), key_blo...]
    all_to_all x2 -> x0, starting transfers between devices: 13.1 us -> none  [the longest x1 6.57 us: body(): lax.all_to_all(summed_out.astype(jnp.bfloat16), 'exp', split_axis=0, conc...]
  transfers between devices with their start and end apart: 5 -> 0, of which waited for: 4 -> 0; matrix products, arithmetic and copies ran while one was open for 23% -> 0% of each run, Pallas kernels for 0% -> 0%
where the time goes in v1:
time: 155 us; the launch traced here: 154 us
  Pallas kernels  143 us (92%)
  local copies, waits for them, and re-layouts  7.98 us (5%)
  other arithmetic  2.5 us (2%)
    pallas_call x1, Pallas kernels, experts(): pl.pallas_call(experts_kernel, out_shape=jax.ShapeDtypeStruct((GROUP, D),...  62.9 us
    pallas_call x1, Pallas kernels, project(): pl.pallas_call(project_kernel, out_shape=jax.ShapeDtypeStruct((16, GROUP,...  37.3 us
    pallas_call x1, Pallas kernels, gather_keys(): pl.pallas_call(keys_kernel, out_shape=(jax.ShapeDtypeStruct((16, TOK, LAT...  27.8 us
    pallas_call x1, Pallas kernels, prefill(): pl.pallas_call(prefill_kernel, grid=(q.shape[0] // tile,), out_shape=jax....  11.1 us
    unnamed x24, local copies, waits for them, and re-layouts  6.58 us
    pallas_call x1, Pallas kernels, decode_attention(): pl.pallas_call(decode_kernel, out_shape=jax.ShapeDtypeStruct((GROUP, HEAD...  3.88 us

profile of v1, /device:TPU:1, one launch (start us, length us, event | category | flops | bytes accessed | tf_op | source)
XLA Modules:
  0.0 154.4 jit_solution(10552696880343098906)
XLA Ops:
  0.6 1.8 %copy.30.kv = bf16[128,576]{1,0:T(8,128)(2,1)} copy(bf16[128,576]{0,1:T(8,128)(2,1)} %param.16) | data formatting | bytes 294912 | tf_op args[1]
  2.4 27.8 %shard_map.158 = (bf16[16,128,576]{2,1,0:T(8,128)(2,1)}, bf16[3584,128]{1,0:T(8,128)(2,1)}, bf16[3584,128]{1,0:T(8,128)(2,1)}, bf16[128,3584]{1,0:T(8,128)(2,1)}) custom-call(bf16[128,576]{1,0:T(8,128)(2,1)} %copy.30.kv, bf16[1,7168,128]{2,1,0:T(8,128)(2,1)} %gate.3, bf16[1,7168,128]{2,1,0:T(8,128)(2,1)} %up.3, bf16[1,128,7168]{2,1,0:T(8,128)(2,1)} %down.3), custom_call_target="tpu_custom_call" | custom-call | tf_op jit(solution)/shard_map/pallas_call | solution.py:210
  30.3 0.7 copy.41
  31.0 3.9 %shard_map.160.vals = bf16[16,1024]{1,0:T(8,128)(2,1)} custom-call(s32[1,16]{1,0:T(1,128)} %pages.1, s32[16]{0:T(128)} %lengths.1, bf16[8,16,576]{2,1,0:T(8,128)(2,1)} %bitcast.20, bf16[16,576]{1,0:T(8,128)(2,1)} %own.1, bf16[128,16,576]{2,1,0:T(8,128)(2,1)} %bitcast.16, bf16[8,512,128]{2,1,0:T(8,128)(2,1)} %w_uv.1), custom_call_target="tpu_custom_call" | custom-call | tf_op jit(solution)/shard_map/pallas_call | solution.py:307
  34.9 1.3 copy.33.w_o
  36.2 37.3 %shard_map.161 = bf16[16,16,448]{2,1,0:T(8,128)(2,1)} custom-call(bf16[16,1024]{1,0:T(8,128)(2,1)} %shard_map.160.vals, bf16[1024,448]{1,0:T(8,128)(2,1)} %copy.33.w_o), custom_call_target="tpu_custom_call" | custom-call | tf_op jit(solution)/shard_map/pallas_call | solution.py:413
  73.4 1.0 convert_bitcast_fusion
  74.5 0.3 copy.34
  74.8 0.2 reshape.49
  75.0 0.2 multiply_reduce_fusion
  75.2 0.1 multiply_convert_fusion.normed
  75.4 0.2 fusion.2
  75.6 0.0 copy-done.8
  75.6 0.1 copy.35
  75.7 0.3 select_reduce_fusion
  76.0 0.1 multiply_divide_fusion
  76.1 0.1 select_reduce_fusion.2
  76.2 0.1 pad.2.clone
  76.3 0.7 maximum_maximum_fusion.shares
  77.0 0.8 copy.40
  77.8 62.9 %shard_map.162 = bf16[16,7168]{1,0:T(8,128)(2,1)} custom-call(bf16[16,7168]{1,0:T(8,128)(2,1)} %copy-done.1, bf16[16,128]{1,0:T(8,128)(2,1)} %maximum_maximum_fusion.shares, f32[14,16,512]{2,1,0:T(8,128)} %bitcast.19, bf16[1,7168,128]{2,1,0:T(8,128)(2,1)} %gate.3, bf16[1,7168,128]{2,1,0:T(8,128)(2,1)} %up.3, bf16[1,128,7168]{2,1,0:T(8,128)(2,1)} %down.3, ...), custom_call_target="tpu_custom_call" | custom-call | tf_op jit(solution)/shard_map/pallas_call | solution.py:599
  140.6 2.0 %copy.31.q = bf16[128,8,576]{2,1,0:T(8,128)(2,1)} copy(bf16[128,8,576]{0,2,1:T(8,128)(2,1)S(1)} %copy-done.2) | data formatting | bytes 2359296 | tf_op args[0]
  142.7 11.1 %shard_map.159 = bf16[128,8,512]{2,1,0:T(8,128)(2,1)} custom-call(bf16[128,8,576]{2,1,0:T(8,128)(2,1)} %copy.31.q, bf16[2048,576]{1,0:T(8,128)(2,1)} %bitcast.17), custom_call_target="tpu_custom_call" | custom-call | tf_op jit(solution)/shard_map/pallas_call | solution.py:251
  153.7 0.7 copy.43
  (21 shorter events, 0.1 us)
Async XLA Ops:
  0.6 74.7 %copy-start = (bf16[7168,16]{0,1:T(8,128)(2,1)S(1)}, bf16[7168,16]{0,1:T(8,128)(2,1)}, u32[]{:S(2)}) copy-start(bf16[7168,16]{0,1:T(8,128)(2,1)} %param.25) | copy-start | bytes 688132
  2.4 27.9 %copy-start.6 = (bf16[16,8,576]{2,1,0:T(8,128)(2,1)S(1)}, bf16[16,8,576]{2,1,0:T(8,128)(2,1)}, u32[]{:S(2)}) copy-start(bf16[16,8,576]{2,1,0:T(8,128)(2,1)} %param.17) | copy-start | bytes 442372
  31.0 3.9 %copy-start.3 = (bf16[1024,448]{0,1:T(8,128)(2,1)S(1)}, bf16[1024,448]{0,1:T(8,128)(2,1)}, u32[]{:S(2)}) copy-start(bf16[1024,448]{0,1:T(8,128)(2,1)} %param.22) | copy-start | bytes 2752516
  36.2 38.8 %copy-start.5 = (bf16[16,7168]{1,0:T(8,128)(2,1)S(1)}, bf16[16,7168]{1,0:T(8,128)(2,1)}, u32[]{:S(2)}) copy-start(bf16[16,7168]{1,0:T(8,128)(2,1)} %param.23) | copy-start | bytes 688132
  73.4 1.8 %copy-start.7 = (bf16[7168]{0:T(1024)(128)(2,1)S(1)}, bf16[7168]{0:T(1024)(128)(2,1)}, u32[]{:S(2)}) copy-start(bf16[7168]{0:T(1024)(128)(2,1)} %param.24) | copy-start | bytes 43012
  74.8 0.8 copy-start.8
  75.4 2.4 %copy-start.1 = (bf16[16,7168]{1,0:T(8,128)(2,1)}, bf16[16,7168]{1,0:T(8,128)(2,1)S(1)}, u32[]{:S(2)}) copy-start(bf16[16,7168]{1,0:T(8,128)(2,1)S(1)} %multiply_convert_fusion.normed) | copy-start | bytes 688132
  77.8 62.9 %copy-start.2 = (bf16[128,8,576]{0,2,1:T(8,128)(2,1)S(1)}, bf16[128,8,576]{0,2,1:T(8,128)(2,1)}, u32[]{:S(2)}) copy-start(bf16[128,8,576]{0,2,1:T(8,128)(2,1)} %param.15) | copy-start | bytes 3538948
  142.6 11.1 %copy-start.4 = (bf16[16,7168]{1,0:T(8,128)(2,1)S(1)}, bf16[16,7168]{1,0:T(8,128)(2,1)}, u32[]{:S(2)}) copy-start(bf16[16,7168]{1,0:T(8,128)(2,1)} %shard_map.162) | copy-start | bytes 688132

commit v2 on v0

v2 whole, which is shorter than its diff:
```python
import functools

import jax
import jax.numpy as jnp
from jax import lax
from jax.experimental import pallas as pl
from jax.experimental.pallas import tpu as pltpu
from jax.sharding import PartitionSpec as P

D = 7168
HALF = D // 2
KVL = 512
LAT = 576
HEADS_DEV = 8
VD = 128
FF = 128
TOK = 128
PAGE = 16
GROUP = 16
COLS = 448
EXT = 128
FAR = 1 << 20

qk_scale = 192.0 ** (-0.5)
neg_big = -1e30
MESH = pl.DeviceIdType.MESH
VMEM = pltpu.VMEM
ANY = pl.ANY
LIMIT = 60 * 1024 * 1024


class Place:
    def __init__(self):
        self.c = lax.axis_index("ctx")
        self.e = lax.axis_index("exp")
        self.z, self.k = self.c // 2, self.c % 2
        x, y = self.e // 4, self.e % 4
        self.a = x + self.k * (y - x)
        self.b = y + self.k * (x - y)

    def exp_of(self, a, b):
        return (a + self.k * (b - a)) * 4 + b + self.k * (a - b)

    def plane(self, a, b):
        return (self.c, self.exp_of(a % 4, b % 4))

    def sibling(self):
        return (self.c + 1 - 2 * self.k, self.e)

    def along_z(self, step):
        return (((self.z + step) % 8) * 2 + self.k, self.e)


def greet(devices):
    barrier = pltpu.get_barrier_semaphore()
    for device in devices:
        pl.semaphore_signal(barrier, inc=1, device_id=device, device_id_type=MESH)
    pl.semaphore_wait(barrier, len(devices))


class Wires:
    def __init__(self, send_sem, recv_sem):
        self.send_sem, self.recv_sem = send_sem, recv_sem
        self.count = 0
        self.open = []

    def copy(self, src, dst, device):
        i = self.count
        self.count += 1
        made = pltpu.make_async_remote_copy(
            src_ref=src,
            dst_ref=dst,
            send_sem=self.send_sem.at[i],
            recv_sem=self.recv_sem.at[i],
            device_id=device,
            device_id_type=MESH,
        )
        made.start()
        self.open.append(made)
        return made

    def drain(self):
        for made in self.open:
            made.wait_send()
        self.open = []


def arrive(copies):
    for made in copies:
        made.wait_recv()


def f32(value):
    return value.astype(jnp.float32)


def bf16(value):
    return value.astype(jnp.bfloat16)


Z_STEPS = (4, 3, -3, 2, -2, 1, -1)
PLANE_STEPS = (
    (2, 2), (2, 1), (2, 3), (1, 2), (3, 2), (1, 1), (1, 3), (3, 1), (3, 3),
    (2, 0), (0, 2), (1, 0), (3, 0), (0, 1), (0, 3),
)
RING_STEPS = (2, 1, 3)
CHUNKS = 2
COPIES = 7 + 1 + 3 + 17 + 15 + 15 + 1 + 7 + 7 + 15 + 1 + 15 + 1 + 6 * CHUNKS + 7 + 7 + 1


def layer_kernel(
    pages, lengths, kv_t, dec_q, dec_kv, x_dec, gain, router_t, routes,
    q_t, w_uv, w_o_t, gate, up, down,
    pref, out,
    keys, cache, v_q, v_uv, v_o, w_in, w_out, latent, vals, parts, blocks, rx_half, red, rx_z,
    spread, rows, sums, rx_sums, marks, mid, rx_mid, made_rows, rx_b, mid_b, rx_a,
    zsum, rx_z2, final, send, recv, load,
):
    place = Place()
    z, k, a, b, c, e = place.z, place.k, place.a, place.b, place.c, place.e
    sibling = place.sibling()
    half = pl.ds(k * HALF, HALF)
    other_half = pl.ds((1 - k) * HALF, HALF)
    loads = []
    for i, (src, dst) in enumerate(
        (
            (w_uv, v_uv),
            (w_o_t, v_o),
            (gate.at[0, half, :], w_in.at[:, pl.ds(0, FF)]),
            (up.at[0, half, :], w_in.at[:, pl.ds(FF, FF)]),
            (down.at[0, :, half], w_out.at[pl.ds(0, FF), :]),
            (q_t, v_q),
        )
    ):
        made = pltpu.make_async_copy(src, dst, load.at[i])
        made.start()
        loads.append(made)
    keys[k, z] = jnp.transpose(kv_t[...])

    source = [pages[0, i] // 8 for i in range(16)]
    rank = []
    for i in range(16):
        before = jnp.int32(0)
        for j in range(i):
            before = before + jnp.where(source[j] == source[i], 1, 0)
        rank.append(before)
    for j in range(2):
        wanted = jnp.int32(0)
        for i in range(16):
            wanted = jnp.where((source[i] == c) & (rank[i] == j), pages[0, i] % 8, wanted)
        page = keys[k, z, 0:PAGE, :]
        for i in range(1, 8):
            page = jnp.where(wanted == i, keys[k, z, i * PAGE : (i + 1) * PAGE, :], page)
        cache[k, z, j * PAGE : (j + 1) * PAGE, :] = page

    greet(
        [sibling]
        + [place.along_z(d) for d in Z_STEPS]
        + [place.plane(a + i, b + j) for i, j in PLANE_STEPS]
    )
    wires = Wires(send, recv)
    mine = cache.at[k, z]
    page_copies = [wires.copy(mine, mine, place.along_z(d)) for d in Z_STEPS]
    swaps = [
        wires.copy(gate.at[0, other_half, :], w_in.at[:, pl.ds(2 * FF, FF)], sibling),
        wires.copy(up.at[0, other_half, :], w_in.at[:, pl.ds(3 * FF, FF)], sibling),
        wires.copy(down.at[0, :, other_half], w_out.at[pl.ds(FF, FF), :], sibling),
    ]

    count = HEADS_DEV * GROUP
    queries = dec_q[...].reshape(count, LAT)
    own = jnp.broadcast_to(f32(dec_kv[...])[:, None, :], (GROUP, HEADS_DEV, LAT))
    own = own.reshape(count, LAT)
    own_score = jnp.sum(f32(queries) * own, axis=1, keepdims=True)
    row = lax.broadcasted_iota(jnp.int32, (count, 1), 0) // HEADS_DEV
    limit = jnp.zeros((count, 1), jnp.int32)
    for i in range(GROUP):
        limit = jnp.where(row == i, lengths[i], limit)
    lane = lax.broadcasted_iota(jnp.int32, (1, 256), 1)
    allowed = []
    for core in (k, 1 - k):
        position = jnp.full((1, 256), FAR, jnp.int32)
        for i in range(16):
            here = ((lane // 32) * 2 + core == source[i]) & ((lane // PAGE) % 2 == rank[i])
            position = jnp.where(here, i * PAGE + lane % PAGE, position)
        allowed.append(position < limit)
    arrive(page_copies)
    to_sibling = wires.copy(cache.at[k], cache.at[k], sibling)
    block = keys.at[k, z]
    to_r = wires.copy(block, block, place.along_z(1))
    to_l = wires.copy(block, block, place.along_z(-1))
    key_copies = [wires.copy(block, block, sibling)]

    def ring_hop(hop, to_r, to_l):
        to_r.wait_recv()
        to_l.wait_recv()
        if hop == 4:
            ref = keys.at[k, (z + 4) % 8]
            key_copies.append(wires.copy(ref, ref, sibling))
            return None, None
        first, second = keys.at[k, (z - hop) % 8], keys.at[k, (z + hop) % 8]
        right, left = first, second
        if hop == 3:
            right = keys.at[k, (z - hop) % 8, pl.ds(0, TOK // 2), :]
            left = keys.at[k, (z + hop) % 8, pl.ds(TOK // 2, TOK // 2), :]
        to_r = wires.copy(right, right, place.along_z(1))
        to_l = wires.copy(left, left, place.along_z(-1))
        key_copies.append(wires.copy(first, first, sibling))
        key_copies.append(wires.copy(second, second, sibling))
        return to_r, to_l

    scores = []
    for i, core in enumerate((k, 1 - k)):
        if i == 1:
            to_sibling.wait_recv()
        cached = cache[core].reshape(256, LAT)
        score = lax.dot_general(
            queries, cached, (((1,), (1,)), ((), ())), preferred_element_type=jnp.float32
        )
        scores.append(jnp.where(allowed[i], score, neg_big))
    top = jnp.maximum(jnp.max(scores[0], axis=1, keepdims=True), own_score)
    top = jnp.maximum(jnp.max(scores[1], axis=1, keepdims=True), top)
    own_weight = jnp.exp((own_score - top) * qk_scale)
    total = own_weight
    mixed = f32(bf16(own_weight)) * own[:, :KVL]
    for i, core in enumerate((k, 1 - k)):
        weights = jnp.where(allowed[i], jnp.exp((scores[i] - top) * qk_scale), 0.0)
        total = total + jnp.sum(weights, axis=1, keepdims=True)
        cached = cache[core].reshape(256, LAT)
        mixed = mixed + jnp.dot(
            bf16(weights), cached[:, :KVL], preferred_element_type=jnp.float32
        )
    mixed = mixed / total
    for i in range(KVL // 128):
        latent[i] = mixed[:, i * 128 : (i + 1) * 128]
    loads[0].wait()
    for h in range(HEADS_DEV):
        every = pl.ds(h, GROUP, stride=HEADS_DEV)
        part = jnp.concatenate([latent[i, every, :] for i in range(KVL // 128)], axis=1)
        part = jnp.dot(bf16(part), v_uv[h], preferred_element_type=jnp.float32)
        vals[e, :, h * VD : (h + 1) * VD] = bf16(part)

    near = [place.plane(a + i, b + j) for i, j in PLANE_STEPS]
    copies = [wires.copy(vals.at[e], vals.at[e], device) for device in near]
    to_r, to_l = ring_hop(1, to_r, to_l)
    loads[1].wait()
    arrive(copies)
    product = lax.dot_general(
        vals[...].reshape(256, HEADS_DEV * VD),
        v_o[...],
        (((1,), (1,)), ((), ())),
        preferred_element_type=jnp.float32,
    )
    parts[...] = bf16(product).reshape(16, GROUP, COLS)
    copies = [wires.copy(parts.at[device[1]], blocks.at[e], device) for device in near]
    blocks[e] = parts[e]
    to_r, to_l = ring_hop(2, to_r, to_l)
    arrive(copies)
    to_sibling = wires.copy(blocks.at[pl.ds((1 - k) * 8, 8)], rx_half, sibling)
    to_sibling.wait_recv()
    red[...] = bf16(f32(blocks[pl.ds(k * 8, 8)]) + f32(rx_half[...]))

    def sum_z(ref, rx):
        copies = []
        for i, d in enumerate(Z_STEPS):
            copies.append(wires.copy(ref.at[(z + d) % 8], rx.at[i], place.along_z(d)))
        total = f32(ref[z])
        for i in range(7):
            copies[i].wait_recv()
            total = total + f32(rx[i])
        return total

    pair = pl.ds((k * 4 + z // 2) * 2 * COLS, 2 * COLS)
    odd = z % 2 == 1
    x_pair, gain_pair = f32(x_dec[:, pair]), f32(gain[:, pair])
    x_own = jnp.where(odd, x_pair[:, COLS:], x_pair[:, :COLS])
    gain_own = jnp.where(odd, gain_pair[:, COLS:], gain_pair[:, :COLS])
    residual = x_own + sum_z(red, rx_z)
    spread[z] = bf16(residual * gain_own)
    copies = [wires.copy(spread.at[z], spread.at[z], place.along_z(d)) for d in Z_STEPS]
    arrive(copies)
    slot = b * 4 + a
    for i in range(8):
        rows[slot, :, i * COLS : (i + 1) * COLS] = spread[i]

    ref = rows.at[slot]
    along_a = [wires.copy(ref, ref, place.plane(a + d, b)) for d in RING_STEPS]
    along_b = [wires.copy(ref, ref, place.plane(a, b + d)) for d in RING_STEPS]
    scaled = rows[slot]
    logits = lax.dot_general(
        scaled, router_t[:, half], (((1,), (1,)), ((), ())), preferred_element_type=jnp.float32
    )
    gain_half = f32(gain[:, half])
    squares = f32(scaled) / gain_half
    squares = jnp.sum(squares * squares, axis=1, keepdims=True)
    lane = lax.broadcasted_iota(jnp.int32, (GROUP, EXT), 1)
    sums[:, 0:16] = logits
    sums[:, 16:EXT] = jnp.broadcast_to(squares, (GROUP, EXT - 16))
    to_sibling = wires.copy(sums, rx_sums, sibling)
    for i, d in zip((1, 2, 0), (1, 3, 2)):
        along_a[i].wait_recv()
        ref = rows.at[b * 4 + (a - d) % 4]
        along_b += [wires.copy(ref, ref, place.plane(a, b + j)) for j in RING_STEPS]
        if i == 1:
            to_sibling.wait_recv()
            both = sums[...] + rx_sums[...]
            scale = lax.rsqrt(both[:, 16:17] / D + 1e-06)
            affinity = jax.nn.sigmoid(both * scale)
            chosen = lane == routes[:, 0:1]
            for t in range(1, routes.shape[1]):
                chosen = chosen | (lane == routes[:, t : t + 1])
            picked = jnp.where(chosen, affinity, 0.0)
            share = 2.5 * picked / jnp.sum(picked, axis=1, keepdims=True)
            marks[slot] = jnp.where(lane == 16, scale, share)
            mark_copies = [wires.copy(marks.at[slot], marks.at[slot], device) for device in near]
    to_r, to_l = ring_hop(3, to_r, to_l)

    key_at = lax.broadcasted_iota(jnp.int32, (1, 16 * TOK), 1)
    key_at = (((key_at // TOK) % 8) * 2 + key_at // (8 * TOK)) * TOK + key_at % TOK

    def prefill_tile(i):
        queries = jnp.concatenate(
            [jnp.transpose(v_q[2 * i]), jnp.transpose(v_q[2 * i + 1])], axis=0
        )
        all_keys = keys[...].reshape(16 * TOK, LAT)
        scores = lax.dot_general(
            queries, all_keys, (((1,), (1,)), ((), ())), preferred_element_type=jnp.float32
        )
        token = c * TOK + lax.broadcasted_iota(jnp.int32, (2 * TOK, 1), 0) % TOK
        scores = jnp.where(key_at <= token, scores, neg_big)
        top = jnp.max(scores, axis=1, keepdims=True)
        weights = jnp.exp((scores - top) * qk_scale)
        total = jnp.sum(weights, axis=1, keepdims=True)
        mixed = jnp.dot(
            bf16(weights), all_keys[:, :KVL], preferred_element_type=jnp.float32
        )
        pref[2 * i : 2 * i + 2] = bf16(mixed / total).reshape(2, TOK, KVL)

    arrive(along_b)
    for made in loads[2:]:
        made.wait()
    arrive(swaps)

    product = jnp.dot(
        rows[...].reshape(256, HALF), w_in[...], preferred_element_type=jnp.float32
    )
    mid[...] = product.reshape(16, GROUP, 4 * FF)
    to_sibling = wires.copy(mid, rx_mid, sibling)
    arrive(mark_copies)
    mark = marks[...].reshape(256, EXT)
    lane = lax.broadcasted_iota(jnp.int32, (256, EXT), 1)
    share = jnp.sum(jnp.where(lane == e, mark, 0.0), axis=1, keepdims=True)
    scale = mark[:, 16:17]
    ring_hop(4, to_r, to_l)
    to_sibling.wait_recv()
    hidden = []
    for s in range(16):
        own, other = mid[s], rx_mid[(s % 4) * 4 + s // 4]
        at = scale[s * GROUP : (s + 1) * GROUP]
        g0 = (own[:, 0:FF] + other[:, 2 * FF : 3 * FF]) * at
        u0 = (own[:, FF : 2 * FF] + other[:, 3 * FF : 4 * FF]) * at
        g1 = (own[:, 2 * FF : 3 * FF] + other[:, 0:FF]) * at
        u1 = (own[:, 3 * FF : 4 * FF] + other[:, FF : 2 * FF]) * at
        h0 = bf16(jax.nn.silu(g0) * u0)
        h1 = bf16(jax.nn.silu(g1) * u1)
        hidden.append(jnp.concatenate([h0, h1], axis=1))
    hidden = jnp.concatenate(hidden, axis=0)
    produced = jnp.dot(hidden, w_out[...], preferred_element_type=jnp.float32) * share
    made_rows[...] = bf16(produced).reshape(16, GROUP, HALF)

    width = HALF // CHUNKS
    first = []
    for i in range(CHUNKS):
        cols = pl.ds(i * width, width)
        for j, d in enumerate(RING_STEPS):
            src = made_rows.at[pl.ds(((b + d) % 4) * 4, 4), :, cols]
            first.append(wires.copy(src, rx_b.at[j, :, :, cols], place.plane(a, b + d)))
    arrive(key_copies)
    for i in range(3):
        prefill_tile(i)
    second = []
    for i in range(CHUNKS):
        cols = slice(i * width, (i + 1) * width)
        arrive(first[3 * i : 3 * i + 3])
        total = f32(made_rows[pl.ds(b * 4, 4), :, cols])
        for j in range(3):
            total = total + f32(rx_b[j, :, :, cols])
        mid_b[:, :, cols] = bf16(total)
        cols = pl.ds(i * width, width)
        for j, d in enumerate(RING_STEPS):
            src = mid_b.at[(a + d) % 4, :, cols]
            second.append(wires.copy(src, rx_a.at[j, :, cols], place.plane(a + d, b)))
    prefill_tile(3)
    arrive(second)
    total = f32(mid_b[a])
    for j in range(3):
        total = total + f32(rx_a[j])
    for i in range(8):
        zsum[i] = bf16(total[:, i * COLS : (i + 1) * COLS])
    final[k, z] = bf16(residual + sum_z(zsum, rx_z2))
    ref = final.at[k, z]
    arrive([wires.copy(ref, ref, place.along_z(d)) for d in Z_STEPS])
    to_sibling = wires.copy(final.at[k], final.at[k], sibling)
    to_sibling.wait_recv()
    for i in range(16):
        out[:, i * COLS : (i + 1) * COLS] = final[i // 8, i % 8]
    wires.drain()


def layer(*args):
    vmem, smem = pl.BlockSpec(memory_space=VMEM), pl.BlockSpec(memory_space=pltpu.SMEM)
    anywhere = pl.BlockSpec(memory_space=ANY)
    half, full = jnp.bfloat16, jnp.float32
    scratch = [
        ((2, 8, TOK, LAT), half),
        ((2, 8, 2 * PAGE, LAT), half),
        ((HEADS_DEV, LAT, TOK), half),
        ((HEADS_DEV, KVL, VD), half),
        ((COLS, HEADS_DEV * VD), half),
        ((HALF, 4 * FF), half),
        ((2 * FF, HALF), half),
        ((KVL // 128, GROUP * HEADS_DEV, 128), full),
        ((16, GROUP, HEADS_DEV * VD), half),
        ((16, GROUP, COLS), half),
        ((16, GROUP, COLS), half),
        ((8, GROUP, COLS), half),
        ((8, GROUP, COLS), half),
        ((7, GROUP, COLS), half),
        ((8, GROUP, COLS), half),
        ((16, GROUP, HALF), half),
        ((GROUP, EXT), full),
        ((GROUP, EXT), full),
        ((16, GROUP, EXT), full),
        ((16, GROUP, 4 * FF), full),
        ((16, GROUP, 4 * FF), full),
        ((16, GROUP, HALF), half),
        ((3, 4, GROUP, HALF), half),
        ((4, GROUP, HALF), half),
        ((3, GROUP, HALF), half),
        ((8, GROUP, COLS), half),
        ((7, GROUP, COLS), half),
        ((2, 8, GROUP, COLS), half),
    ]
    return pl.pallas_call(
        layer_kernel,
        out_shape=(
            jax.ShapeDtypeStruct((HEADS_DEV, TOK, KVL), half),
            jax.ShapeDtypeStruct((GROUP, D), half),
        ),
        in_specs=[smem] * 2 + [vmem] * 7 + [anywhere] * 6,
        out_specs=[vmem] * 2,
        scratch_shapes=[VMEM(shape, dtype) for shape, dtype in scratch]
        + [
            pltpu.SemaphoreType.DMA((COPIES,)),
            pltpu.SemaphoreType.DMA((COPIES,)),
            pltpu.SemaphoreType.DMA((6,)),
        ],
        compiler_params=pltpu.CompilerParams(
            collective_id=1, has_side_effects=True, vmem_limit_bytes=LIMIT
        ),
    )(*args)


def body(
    q_pref,
    kv_pref,
    dec_q,
    dec_kv,
    page_req,
    dec_len,
    w_uv,
    w_o,
    x_dec,
    norm_gain,
    router,
    routes,
    w_gate,
    w_up,
    w_down,
):
    pref, decode_out = layer(
        page_req,
        dec_len,
        kv_pref.T,
        dec_q,
        dec_kv,
        x_dec,
        norm_gain.reshape(1, D),
        router.T,
        routes,
        jnp.transpose(q_pref, (1, 2, 0)),
        w_uv,
        w_o.T,
        w_gate,
        w_up,
        w_down,
    )
    return (jnp.swapaxes(pref, 0, 1), decode_out)


def solution(mesh):
    placed = (
        P("ctx", "exp", None),
        P("ctx", None),
        P("exp", "ctx", None),
        P("exp", None),
        P("exp", None),
        P("exp"),
        P("ctx", None, None),
        P("ctx", "exp"),
        P("exp", None),
        P(),
        P(),
        P("exp", None),
        P("exp", None, "ctx"),
        P("exp", None, "ctx"),
        P("exp", "ctx", None),
    )
    return jax.shard_map(
        body,
        mesh=mesh,
        in_specs=placed,
        out_specs=(P("ctx", "exp", None), P("exp", None)),
        check_vma=False,
    )
```

time: 542 us -> 111 us (0.20)
  waiting for transfers between devices: 260 us -> 0 us
  Pallas kernels: 0 us -> 104 us
  matrix products: 102 us -> 0 us
  blocking collectives: 88.6 us -> 0 us
  local copies, waits for them, and re-layouts: 43.1 us -> 6.2 us
  between operations: 14.1 us -> 0.65 us
  starting transfers between devices: 13.4 us -> 0 us
  loops' own time: 9.68 us -> 0 us
  other arithmetic: 9 us -> 0 us
    psum x2 -> x0, waiting for transfers between devices: 219 us -> none  [the longest x1 110 us: body(): lax.psum(partial_out.astype(jnp.bfloat16), 'ctx').astype(jnp.float32)]
    pallas_call x0 -> x1, Pallas kernels: none -> 104 us  [layer(): pl.pallas_call(layer_kernel, out_shape=(jax.ShapeDtypeStruct((HEADS_DEV,...]
    dot_general x42 -> x0, matrix products: 102 us -> none  [the longest x16 54.6 us: key_step(): jnp.dot(weights.astype(jnp.bfloat16), key_block[:, :value_width], preferr...]
    all_to_all x1 -> x0, blocking collectives: 46.6 us -> none  [body(): lax.all_to_all(outgoing_rows, 'exp', split_axis=0, concat_axis=0, tiled=T...]
    all_gather x2 -> x0, blocking collectives: 42 us -> none  [the longest x1 22.9 us: body(): arrived = lax.all_gather(outgoing, 'ctx', axis=0, tiled=True)]
    all_gather x1 -> x0, waiting for transfers between devices: 33 us -> none  [body(): key_piece = lax.all_gather(kv_pref, 'ctx', axis=0, tiled=True)]
    squeeze x16 -> x0, local copies, waits for them, and re-layouts: 15 us -> none  [body(): lax.scan(key_step, carry_state, (jnp.arange(key_blocks.shape[0]), key_blo...]
    all_to_all x2 -> x0, starting transfers between devices: 13.1 us -> none  [the longest x1 6.57 us: body(): lax.all_to_all(summed_out.astype(jnp.bfloat16), 'exp', split_axis=0, conc...]
  transfers between devices with their start and end apart: 5 -> 0, of which waited for: 4 -> 0; matrix products, arithmetic and copies ran while one was open for 23% -> 0% of each run, Pallas kernels for 0% -> 0%
where the time goes in v2:
time: 111 us
  Pallas kernels  104 us (94%)
  local copies, waits for them, and re-layouts  6.2 us (6%)
    pallas_call x1, Pallas kernels, layer(): pl.pallas_call(layer_kernel, out_shape=(jax.ShapeDtypeStruct((HEADS_DEV,...  104 us
    unnamed x5, local copies, waits for them, and re-layouts  4.86 us

profile of v2, /device:TPU:1, one launch (start us, length us, event | category | flops | bytes accessed | tf_op | source)
XLA Modules:
  0.0 111.1 jit_solution(755386466278821496)
XLA Ops:
  0.6 1.4 %copy.17.routes = s32[16,8]{1,0:T(8,128)} copy(s32[16,8]{0,1:T(8,128)} %param.26) | data formatting | bytes 1024 | tf_op args[11]
  2.0 1.3 %reshape.7.gain = bf16[1,7168]{1,0:T(2,128)(2,1)} reshape(bf16[7168]{0:T(1024)(128)(2,1)} %param.24) | data formatting | bytes 28672 | tf_op jit(solution)/shard_map/reshape | solution.py:488
  3.3 104.2 %shard_map.158 = (bf16[8,128,512]{2,1,0:T(8,128)(2,1)}, bf16[16,7168]{1,0:T(8,128)(2,1)}) custom-call(s32[1,16]{1,0:T(1,128)} %pages.1, s32[16]{0:T(128)} %lengths.1, bf16[576,128]{1,0:T(8,128)(2,1)} %bitcast.9, bf16[16,8,576]{2,1,0:T(8,128)(2,1)} %dec_q.1, bf16[16,576]{1,0:T(8,128)(2,1)} %dec_kv.1, bf16[16,7168]{1,0:T(8,128)(2,1)} %x_dec.1, ...), custom_call_target="tpu_custom_call" | custom-call | tf_op jit(solution)/shard_map/pallas_call | solution.py:444
  107.5 0.0 copy-start
  107.6 2.8 %copy.18 = bf16[128,8,512]{2,1,0:T(8,128)(2,1)} copy(bf16[128,8,512]{2,0,1:T(8,128)(2,1)} %bitcast.6) | data formatting | bytes 2097152
  110.4 0.0 copy-done
  110.4 0.7 copy.20
Async XLA Ops:
  107.5 2.8 %copy-start = (bf16[16,7168]{1,0:T(8,128)(2,1)S(1)}, bf16[16,7168]{1,0:T(8,128)(2,1)}, u32[]{:S(2)}) copy-start(bf16[16,7168]{1,0:T(8,128)(2,1)} %get-tuple-element.11) | copy-start | bytes 688132

commit v3 on v2

v3 whole, which is shorter than its diff:
```python
import functools

import jax
import jax.numpy as jnp
from jax import lax
from jax.experimental import pallas as pl
from jax.experimental.pallas import tpu as pltpu
from jax.sharding import PartitionSpec as P

D = 7168
HALF = D // 2
KVL = 512
LAT = 576
HEADS_DEV = 8
VD = 128
FF = 128
TOK = 128
PAGE = 16
GROUP = 16
COLS = 448
EXT = 128
FAR = 1 << 20

qk_scale = 192.0 ** (-0.5)
neg_big = -1e30
MESH = pl.DeviceIdType.MESH
VMEM = pltpu.VMEM
ANY = pl.ANY
LIMIT = 60 * 1024 * 1024


class Place:
    def __init__(self):
        self.c = lax.axis_index("ctx")
        self.e = lax.axis_index("exp")
        self.z, self.k = self.c // 2, self.c % 2
        x, y = self.e // 4, self.e % 4
        self.a = x + self.k * (y - x)
        self.b = y + self.k * (x - y)

    def exp_of(self, a, b):
        return (a + self.k * (b - a)) * 4 + b + self.k * (a - b)

    def plane(self, a, b):
        return (self.c, self.exp_of(a % 4, b % 4))

    def sibling(self):
        return (self.c + 1 - 2 * self.k, self.e)

    def along_z(self, step):
        return (((self.z + step) % 8) * 2 + self.k, self.e)


def greet(devices):
    barrier = pltpu.get_barrier_semaphore()
    for device in devices:
        pl.semaphore_signal(barrier, inc=1, device_id=device, device_id_type=MESH)
    return lambda: pl.semaphore_wait(barrier, len(devices))


class Wires:
    def __init__(self, send_sem, recv_sem):
        self.send_sem, self.recv_sem = send_sem, recv_sem
        self.count = 0
        self.open = []

    def copy(self, src, dst, device):
        i = self.count
        self.count += 1
        made = pltpu.make_async_remote_copy(
            src_ref=src,
            dst_ref=dst,
            send_sem=self.send_sem.at[i],
            recv_sem=self.recv_sem.at[i],
            device_id=device,
            device_id_type=MESH,
        )
        made.start()
        self.open.append(made)
        return made

    def drain(self):
        for made in self.open:
            made.wait_send()
        self.open = []


def arrive(copies):
    for made in copies:
        made.wait_recv()


def f32(value):
    return value.astype(jnp.float32)


def bf16(value):
    return value.astype(jnp.bfloat16)


Z_STEPS = (4, 3, -3, 2, -2, 1, -1)
PLANE_STEPS = (
    (2, 2), (2, 1), (2, 3), (1, 2), (3, 2), (1, 1), (1, 3), (3, 1), (3, 3),
    (2, 0), (0, 2), (1, 0), (3, 0), (0, 1), (0, 3),
)
RING_STEPS = (2, 1, 3)
PLACES = (0, 1, -1, -2, 2, -3, 3, 4)
PARTS = ((4, 2), (0, 4))
SUM_PARTS = ((0, 4), (4, 2))
COPIES = 7 + 1 + 17 + 17 + 15 + 15 + 1 + 7 + 12 + 30 + 8 + 1 + 15 + 1 + 8 + 12 + 5 + 7 + 1
LOADS = HEADS_DEV + 5 + 16 + 1 + 1


def layer_kernel(
    pages, lengths, kv_t, dec_q, dec_kv,
    x_dec_in, gain_in, router_in, routes_in, q_t, w_uv, w_o_t, gate, up, down,
    pref, out,
    x_dec, gain_rows, gain, router_t, routes, keys, keys_t, cache, v_q, v_uv, v_o, w_in, w_out, latent, vals, parts, blocks, rx_half, red, rx_z,
    rows, sums, rx_sums, marks, by_token, pref_rows, scores_at, weights_at, totals, mid, rx_mid, made_rows, rx_pre, rx_b, mid_b, rx_a,
    zsum, rx_z2, final, send, recv, load,
):
    place = Place()
    z, k, a, b, c, e = place.z, place.k, place.a, place.b, place.c, place.e
    sibling = place.sibling()
    half = pl.ds(k * HALF, HALF)
    other_half = pl.ds((1 - k) * HALF, HALF)
    def block_copies(side, at):
        pairs = []
        for p, d in enumerate(PLACES):
            block = pl.ds((side * 8 + (z + d) % 8) * COLS, COLS)
            pairs.append((gate.at[0, block, :], w_in.at[p, :, pl.ds(at * FF, FF)]))
            pairs.append((up.at[0, block, :], w_in.at[p, :, pl.ds((at + 1) * FF, FF)]))
        return pairs

    enter = greet(
        [sibling]
        + [place.along_z(d) for d in Z_STEPS]
        + [place.plane(a + i, b + j) for i, j in PLANE_STEPS]
    )
    loads = []
    for i, (src, dst) in enumerate(
        [(w_uv.at[h], v_uv.at[:, pl.ds(h * VD, VD)]) for h in range(HEADS_DEV)]
        + [
            (w_o_t, v_o),
            (x_dec_in, x_dec),
            (gain_in, gain_rows),
            (router_in, router_t),
            (routes_in, routes),
        ]
        + block_copies(k, 0)
        + [(down.at[0, :, half], w_out.at[pl.ds(0, FF), :]), (q_t, v_q)]
    ):
        made = pltpu.make_async_copy(src, dst, load.at[i])
        made.start()
        loads.append(made)
    keys[k, z] = jnp.transpose(kv_t[...])

    source = [pages[0, i] // 8 for i in range(16)]
    rank = []
    for i in range(16):
        before = jnp.int32(0)
        for j in range(i):
            before = before + jnp.where(source[j] == source[i], 1, 0)
        rank.append(before)
    for j in range(2):
        wanted = jnp.int32(0)
        for i in range(16):
            wanted = jnp.where((source[i] == c) & (rank[i] == j), pages[0, i] % 8, wanted)
        page = keys[k, z, 0:PAGE, :]
        for i in range(1, 8):
            page = jnp.where(wanted == i, keys[k, z, i * PAGE : (i + 1) * PAGE, :], page)
        cache[k, z, j * PAGE : (j + 1) * PAGE, :] = page

    enter()
    wires = Wires(send, recv)
    mine = cache.at[k, z]
    page_copies = [wires.copy(mine, mine, place.along_z(d)) for d in Z_STEPS]
    swaps = [wires.copy(src, dst, sibling) for src, dst in block_copies(1 - k, 2)]
    swaps.append(wires.copy(down.at[0, :, other_half], w_out.at[pl.ds(FF, FF), :], sibling))

    count = HEADS_DEV * GROUP
    queries = dec_q[...].reshape(count, LAT)
    own = jnp.broadcast_to(f32(dec_kv[...])[:, None, :], (GROUP, HEADS_DEV, LAT))
    own = own.reshape(count, LAT)
    own_score = jnp.sum(f32(queries) * own, axis=1, keepdims=True)
    row = lax.broadcasted_iota(jnp.int32, (count, 1), 0) // HEADS_DEV
    limit = jnp.zeros((count, 1), jnp.int32)
    for i in range(GROUP):
        limit = jnp.where(row == i, lengths[i], limit)
    lane = lax.broadcasted_iota(jnp.int32, (1, 256), 1)
    allowed = []
    for core in (k, 1 - k):
        position = jnp.full((1, 256), FAR, jnp.int32)
        for i in range(16):
            here = ((lane // 32) * 2 + core == source[i]) & ((lane // PAGE) % 2 == rank[i])
            position = jnp.where(here, i * PAGE + lane % PAGE, position)
        allowed.append(position < limit)
    arrive(page_copies)
    to_sibling = wires.copy(cache.at[k], cache.at[k], sibling)
    block = keys.at[k, z]
    to_r = wires.copy(block, block, place.along_z(1))
    to_l = wires.copy(block, block, place.along_z(-1))
    key_copies = [wires.copy(block, block, sibling)]

    def ring_hop(hop, to_r, to_l):
        to_r.wait_recv()
        to_l.wait_recv()
        if hop == 4:
            ref = keys.at[k, (z + 4) % 8]
            key_copies.append(wires.copy(ref, ref, sibling))
            return None, None
        first, second = keys.at[k, (z - hop) % 8], keys.at[k, (z + hop) % 8]
        right, left = first, second
        if hop == 3:
            right = keys.at[k, (z - hop) % 8, pl.ds(0, TOK // 2), :]
            left = keys.at[k, (z + hop) % 8, pl.ds(TOK // 2, TOK // 2), :]
        to_r = wires.copy(right, right, place.along_z(1))
        to_l = wires.copy(left, left, place.along_z(-1))
        key_copies.append(wires.copy(first, first, sibling))
        key_copies.append(wires.copy(second, second, sibling))
        return to_r, to_l

    scores = []
    for i, core in enumerate((k, 1 - k)):
        if i == 1:
            to_sibling.wait_recv()
        cached = cache[core].reshape(256, LAT)
        score = lax.dot_general(
            queries, cached, (((1,), (1,)), ((), ())), preferred_element_type=jnp.float32
        )
        scores.append(jnp.where(allowed[i], score, neg_big))
    top = jnp.maximum(jnp.max(scores[0], axis=1, keepdims=True), own_score)
    top = jnp.maximum(jnp.max(scores[1], axis=1, keepdims=True), top)
    own_weight = jnp.exp((own_score - top) * qk_scale)
    total = own_weight
    mixed = f32(bf16(own_weight)) * own[:, :KVL]
    for i, core in enumerate((k, 1 - k)):
        weights = jnp.where(allowed[i], jnp.exp((scores[i] - top) * qk_scale), 0.0)
        total = total + jnp.sum(weights, axis=1, keepdims=True)
        cached = cache[core].reshape(256, LAT)
        mixed = mixed + jnp.dot(
            bf16(weights), cached[:, :KVL], preferred_element_type=jnp.float32
        )
    for made in loads[:HEADS_DEV]:
        made.wait()
    product = jnp.dot(bf16(mixed / total), v_uv[...], preferred_element_type=jnp.float32)
    for h in range(HEADS_DEV):
        latent[h] = product[:, h * VD : (h + 1) * VD]
        part = latent[h, pl.ds(h, GROUP, stride=HEADS_DEV), :]
        vals[e, :, h * VD : (h + 1) * VD] = bf16(part)

    near = [place.plane(a + i, b + j) for i, j in PLANE_STEPS]
    copies = [wires.copy(vals.at[e], vals.at[e], device) for device in near]
    to_r, to_l = ring_hop(1, to_r, to_l)
    for made in loads[HEADS_DEV : HEADS_DEV + 5]:
        made.wait()
    for i in range(D // 128):
        gain[:, i * 128 : (i + 1) * 128] = f32(gain_rows[i : i + 1, :])
    arrive(copies)
    product = lax.dot_general(
        vals[...].reshape(256, HEADS_DEV * VD),
        v_o[...],
        (((1,), (1,)), ((), ())),
        preferred_element_type=jnp.float32,
    )
    parts[...] = bf16(product).reshape(16, GROUP, COLS)
    copies = [wires.copy(parts.at[device[1]], blocks.at[e], device) for device in near]
    blocks[e] = parts[e]
    to_r, to_l = ring_hop(2, to_r, to_l)
    arrive(copies)
    to_sibling = wires.copy(blocks.at[pl.ds((1 - k) * 8, 8)], rx_half, sibling)
    to_sibling.wait_recv()
    red[...] = bf16(f32(blocks[pl.ds(k * 8, 8)]) + f32(rx_half[...]))

    def sum_z(ref, rx, meanwhile):
        copies = []
        for i, d in enumerate(Z_STEPS):
            copies.append(wires.copy(ref.at[(z + d) % 8], rx.at[i], place.along_z(d)))
        total = f32(ref[z])
        meanwhile()
        for i in range(7):
            copies[i].wait_recv()
            total = total + f32(rx[i])
        return total

    pair = pl.ds((k * 4 + z // 2) * 2 * COLS, 2 * COLS)
    odd = z % 2 == 1
    x_pair, gain_pair, router_pair = f32(x_dec[:, pair]), gain[:, pair], f32(router_t[:, pair])
    x_own = jnp.where(odd, x_pair[:, COLS:], x_pair[:, :COLS])
    gain_own = jnp.where(odd, gain_pair[:, COLS:], gain_pair[:, :COLS])
    router_own = jnp.where(odd, router_pair[:, COLS:], router_pair[:, :COLS])
    ring = []
    residual = x_own + sum_z(red, rx_z, lambda: ring.extend(ring_hop(3, to_r, to_l)))
    scaled = bf16(residual * gain_own)
    slot = b * 4 + a
    rows[0, slot] = scaled
    spread = {}
    for p in (5, 4, 3, 1, 2):
        spread[p] = wires.copy(rows.at[0, slot], rows.at[p, slot], place.along_z(-PLACES[p]))

    ring_hop(4, *ring)

    lane = lax.broadcasted_iota(jnp.int32, (GROUP, EXT), 1)
    sums[z, :, 0:16] = lax.dot_general(
        scaled, bf16(router_own), (((1,), (1,)), ((), ())), preferred_element_type=jnp.float32
    )
    squares = jnp.sum(residual * residual, axis=1, keepdims=True)
    sums[z, :, 16:EXT] = jnp.broadcast_to(squares, (GROUP, EXT - 16))

    along_a, along_b = [], []

    def send_part(part):
        first, size = PARTS[part]
        for p in range(first, first + size):
            if p > 0:
                spread[p].wait_recv()
        ref = rows.at[pl.ds(first, size), slot]
        along_a.append([wires.copy(ref, ref, place.plane(a + d, b)) for d in RING_STEPS])
        along_b.append([wires.copy(ref, ref, place.plane(a, b + d)) for d in RING_STEPS])

    def pass_part(part):
        first, size = PARTS[part]
        for i, d in zip((1, 2, 0), (1, 3, 2)):
            along_a[part][i].wait_recv()
            ref = rows.at[pl.ds(first, size), b * 4 + (a - d) % 4]
            along_b[part] += [wires.copy(ref, ref, place.plane(a, b + j)) for j in RING_STEPS]

    passed = []

    def pass_z(j):
        group = pl.ds(((b + j) % 4) * 4, 4)
        for p, q, d in ((4, 6, -1), (5, 7, 1)):
            passed.append(wires.copy(rows.at[p, group], rows.at[q, group], place.along_z(d)))

    def pass_z_from(step):
        arrive(along_b[0][RING_STEPS.index(step) :: 3])
        pass_z(-step)

    send_part(0)
    send_part(1)
    sum_copies = [wires.copy(sums.at[z], sums.at[z], place.along_z(d)) for d in Z_STEPS]
    arrive(key_copies)
    for i in range(16):
        block = keys[i // 8, i % 8, :, 0:KVL]
        keys_t[:, i * TOK : (i + 1) * TOK] = jnp.transpose(block)
    loads[-1].wait()
    pass_part(0)
    pass_z(0)
    pass_part(1)
    arrive(sum_copies)
    total = sums[0]
    for i in range(1, 8):
        total = total + sums[i]
    rx_sums[k] = total
    to_sibling = wires.copy(rx_sums.at[k], rx_sums.at[k], sibling)
    pass_z_from(1)
    pass_z_from(3)
    to_sibling.wait_recv()
    both = rx_sums[0] + rx_sums[1]
    scale = lax.rsqrt(both[:, 16:17] / D + 1e-06)
    affinity = jax.nn.sigmoid(both * scale)
    itself = lax.broadcasted_iota(jnp.int32, (GROUP, GROUP), 0) == lax.broadcasted_iota(
        jnp.int32, (GROUP, GROUP), 1
    )
    chosen = lane < 0
    for t in range(routes.shape[0]):
        named = jnp.sum(jnp.where(itself, routes[t : t + 1, :], 0), axis=1, keepdims=True)
        chosen = chosen | (lane == named)
    picked = jnp.where(chosen, affinity, 0.0)
    share = 2.5 * picked / jnp.sum(picked, axis=1, keepdims=True)
    mark = jnp.where(lane == 16, scale, share)
    marks[slot] = jnp.where(lane[0:8] < 32, mark[0:8], pltpu.roll(mark[8:16], 32, 1))
    mark_copies = [wires.copy(marks.at[slot], marks.at[slot], device) for device in near]
    pass_z_from(2)
    def score_tile(i):
        queries = jnp.concatenate([v_q[2 * i], v_q[2 * i + 1]], axis=1)
        scores_at[i] = jnp.dot(
            keys[...].reshape(16 * TOK, LAT), queries, preferred_element_type=jnp.float32
        )

    def weigh_tile(i):
        shape = (TOK, 2 * TOK)
        ahead = lax.broadcasted_iota(jnp.int32, shape, 0)
        ahead = ahead - lax.broadcasted_iota(jnp.int32, shape, 1) % TOK

        def block(n):
            behind = (c - (n % 8) * 2 - n // 8) * TOK
            return jnp.where(ahead <= behind, scores_at[i, n * TOK : (n + 1) * TOK], neg_big)

        top = block(0)
        for n in range(1, 16):
            top = jnp.maximum(top, block(n))
        top = jnp.max(top, axis=0, keepdims=True)
        total = 0.0
        for n in range(16):
            weights = jnp.exp((block(n) - top) * qk_scale)
            total = total + weights
            weights_at[i, n * TOK : (n + 1) * TOK] = bf16(weights)
        totals[i : i + 1] = jnp.sum(total, axis=0, keepdims=True)

    def mix_tile(i):
        mixed = jnp.dot(keys_t[...], weights_at[i], preferred_element_type=jnp.float32)
        mixed = mixed / totals[i : i + 1]
        for j in range(2):
            head = jnp.transpose(mixed[:, j * TOK : (j + 1) * TOK])
            every = pl.ds(2 * i + j, TOK, stride=HEADS_DEV)
            for t in range(KVL // 128):
                by_token[t, every, :] = head[:, t * 128 : (t + 1) * 128]

    score_tile(0)
    score_tile(1)
    arrive(along_b[1])
    for made in loads[HEADS_DEV + 5 : -1]:
        made.wait()
    arrive(swaps)

    def product_of(places):
        total = 0.0
        for p in places:
            block = rows[p].reshape(256, COLS)
            total = total + jnp.dot(block, w_in[p], preferred_element_type=jnp.float32)
        return total

    mid[...] = product_of(range(6)).reshape(16, GROUP, 4 * FF)
    arrive(passed)
    product = mid[...].reshape(256, 4 * FF) + product_of((6, 7))
    mid[...] = product.reshape(16, GROUP, 4 * FF)
    to_sibling = wires.copy(mid, rx_mid, sibling)
    arrive(mark_copies)
    mark = marks[...].reshape(128, EXT)
    lane = lax.broadcasted_iota(jnp.int32, (128, EXT), 1)

    def mark_at(at):
        low = jnp.sum(jnp.where(lane == at, mark, 0.0), axis=1, keepdims=True)
        high = jnp.sum(jnp.where(lane == at + 32, mark, 0.0), axis=1, keepdims=True)
        both = [low.reshape(16, 1, 8, 1), high.reshape(16, 1, 8, 1)]
        return jnp.concatenate(both, axis=1).reshape(256, 1)

    share, scale = mark_at(e), mark_at(16)
    weigh_tile(0)
    to_sibling.wait_recv()
    hidden = []
    for s in range(16):
        own, other = mid[s], rx_mid[(s % 4) * 4 + s // 4]
        at = scale[s * GROUP : (s + 1) * GROUP]
        g0 = (own[:, 0:FF] + other[:, 2 * FF : 3 * FF]) * at
        u0 = (own[:, FF : 2 * FF] + other[:, 3 * FF : 4 * FF]) * at
        g1 = (own[:, 2 * FF : 3 * FF] + other[:, 0:FF]) * at
        u1 = (own[:, 3 * FF : 4 * FF] + other[:, FF : 2 * FF]) * at
        h0 = bf16(jax.nn.silu(g0) * u0)
        h1 = bf16(jax.nn.silu(g1) * u1)
        hidden.append(jnp.concatenate([h0, h1], axis=1))
    hidden = jnp.concatenate(hidden, axis=0)
    produced = jnp.dot(hidden, w_out[...], preferred_element_type=jnp.float32) * share
    for i in range(8):
        at = jnp.int32(0)
        for p, d in enumerate(PLACES):
            at = jnp.where((z + d - i) % 8 == 0, p, at)
        made_rows[at] = bf16(produced[:, i * COLS : (i + 1) * COLS]).reshape(16, GROUP, COLS)

    early = []
    for step in (2, 1, 3, 0):
        group = pl.ds(((b + step) % 4) * 4, 4)
        for p, d in ((6, 1), (7, -1)):
            src, dst = made_rows.at[p, group], rx_pre.at[p - 6, group]
            early.append(wires.copy(src, dst, place.along_z(d)))
    first, second = [], []

    def sum_b(part, j):
        start, size = SUM_PARTS[part]
        group = pl.ds(((b + RING_STEPS[j]) % 4) * 4, 4)
        src, dst = made_rows.at[pl.ds(start, size), group], rx_b.at[j, pl.ds(start, size)]
        first.append(wires.copy(src, dst, place.plane(a, b + RING_STEPS[j])))

    def sum_a(part):
        start, size = SUM_PARTS[part]
        arrive(first[3 * part : 3 * part + 3])
        at = slice(start, start + size)
        total = f32(made_rows[at, pl.ds(b * 4, 4)])
        for j in range(3):
            total = total + f32(rx_b[j, at])
        mid_b[at] = bf16(total)
        for j, d in enumerate(RING_STEPS):
            src = mid_b.at[pl.ds(start, size), (a + d) % 4]
            dst = rx_a.at[j, pl.ds(start, size)]
            second.append(wires.copy(src, dst, place.plane(a + d, b)))

    for j in range(3):
        sum_b(0, j)
    weigh_tile(1)
    mix_tile(0)
    score_tile(2)
    for j, step in enumerate((2, 1, 3, 0)):
        arrive(early[2 * j : 2 * j + 2])
        group = pl.ds(((b + step) % 4) * 4, 4)
        for i in range(2):
            total = f32(made_rows[4 + i, group]) + f32(rx_pre[i, group])
            made_rows[4 + i, group] = bf16(total)
        if j < 3:
            sum_b(1, j)
    sum_a(0)
    sum_a(1)
    weigh_tile(2)
    mix_tile(1)
    arrive(second)
    total = f32(mid_b[:, a])
    for j in range(3):
        total = total + f32(rx_a[j])
    zsum[...] = bf16(total)
    copies = []
    for p in (5, 4, 3, 2, 1):
        copies.append(wires.copy(zsum.at[p], rx_z2.at[p - 1], place.along_z(PLACES[p])))
    total = residual + total[0]
    mix_tile(2)
    score_tile(3)
    weigh_tile(3)
    arrive(copies)
    for i in range(5):
        total = total + f32(rx_z2[i])
    final[k, z] = bf16(total)
    ref = final.at[k, z]
    copies = [wires.copy(ref, ref, place.along_z(d)) for d in Z_STEPS]
    mix_tile(3)
    for t in range(KVL // 128):
        at = slice(t * 128, (t + 1) * 128)
        pref_rows[:, :, at] = bf16(by_token[t].reshape(TOK, HEADS_DEV, 128))
    pref_copy = pltpu.make_async_copy(pref_rows, pref, load.at[LOADS])
    pref_copy.start()
    arrive(copies)
    to_sibling = wires.copy(final.at[k], final.at[k], sibling)
    to_sibling.wait_recv()
    for i in range(16):
        out[:, i * COLS : (i + 1) * COLS] = final[i // 8, i % 8]
    pref_copy.wait()
    wires.drain()


def layer(*args):
    vmem, smem = pl.BlockSpec(memory_space=VMEM), pl.BlockSpec(memory_space=pltpu.SMEM)
    anywhere = pl.BlockSpec(memory_space=ANY)
    half, full = jnp.bfloat16, jnp.float32
    scratch = [
        ((GROUP, D), half),
        ((D // 128, 128), half),
        ((1, D), full),
        ((16, D), half),
        ((8, GROUP), jnp.int32),
        ((2, 8, TOK, LAT), half),
        ((KVL, 16 * TOK), half),
        ((2, 8, 2 * PAGE, LAT), half),
        ((HEADS_DEV, LAT, TOK), half),
        ((KVL, HEADS_DEV * VD), half),
        ((COLS, HEADS_DEV * VD), half),
        ((8, COLS, 4 * FF), half),
        ((2 * FF, HALF), half),
        ((HEADS_DEV, GROUP * HEADS_DEV, VD), full),
        ((16, GROUP, HEADS_DEV * VD), half),
        ((16, GROUP, COLS), half),
        ((16, GROUP, COLS), half),
        ((8, GROUP, COLS), half),
        ((8, GROUP, COLS), half),
        ((7, GROUP, COLS), half),
        ((8, 16, GROUP, COLS), half),
        ((8, GROUP, EXT), full),
        ((2, GROUP, EXT), full),
        ((16, 8, EXT), full),
        ((KVL // 128, TOK * HEADS_DEV, 128), full),
        ((TOK, HEADS_DEV, KVL), half),
        ((4, 16 * TOK, 2 * TOK), full),
        ((4, 16 * TOK, 2 * TOK), half),
        ((8, 2 * TOK), full),
        ((16, GROUP, 4 * FF), full),
        ((16, GROUP, 4 * FF), full),
        ((8, 16, GROUP, COLS), half),
        ((2, 16, GROUP, COLS), half),
        ((3, 6, 4, GROUP, COLS), half),
        ((6, 4, GROUP, COLS), half),
        ((3, 6, GROUP, COLS), half),
        ((6, GROUP, COLS), half),
        ((5, GROUP, COLS), half),
        ((2, 8, GROUP, COLS), half),
    ]
    return pl.pallas_call(
        layer_kernel,
        out_shape=(
            jax.ShapeDtypeStruct((TOK, HEADS_DEV, KVL), half),
            jax.ShapeDtypeStruct((GROUP, D), half),
        ),
        in_specs=[smem] * 2 + [vmem] * 3 + [anywhere] * 10,
        out_specs=[anywhere, vmem],
        scratch_shapes=[VMEM(shape, dtype) for shape, dtype in scratch]
        + [
            pltpu.SemaphoreType.DMA((COPIES,)),
            pltpu.SemaphoreType.DMA((COPIES,)),
            pltpu.SemaphoreType.DMA((LOADS + 1,)),
        ],
        compiler_params=pltpu.CompilerParams(
            collective_id=1, has_side_effects=True, vmem_limit_bytes=LIMIT
        ),
    )(*args)


def body(
    q_pref,
    kv_pref,
    dec_q,
    dec_kv,
    page_req,
    dec_len,
    w_uv,
    w_o,
    x_dec,
    norm_gain,
    router,
    routes,
    w_gate,
    w_up,
    w_down,
):
    pref, decode_out = layer(
        page_req,
        dec_len,
        kv_pref.T,
        dec_q,
        dec_kv,
        x_dec,
        norm_gain.reshape(D // 128, 128),
        router.T,
        routes.T,
        jnp.transpose(q_pref, (1, 2, 0)),
        w_uv,
        w_o.T,
        w_gate,
        w_up,
        w_down,
    )
    return (pref, decode_out)


def solution(mesh):
    placed = (
        P("ctx", "exp", None),
        P("ctx", None),
        P("exp", "ctx", None),
        P("exp", None),
        P("exp", None),
        P("exp"),
        P("ctx", None, None),
        P("ctx", "exp"),
        P("exp", None),
        P(),
        P(),
        P("exp", None),
        P("exp", None, "ctx"),
        P("exp", None, "ctx"),
        P("exp", "ctx", None),
    )
    return jax.shard_map(
        body,
        mesh=mesh,
        in_specs=placed,
        out_specs=(P("ctx", "exp", None), P("exp", None)),
        check_vma=False,
    )
```

time: 111 us -> 101 us (0.910)
  Pallas kernels: 104 us -> 97 us
  local copies, waits for them, and re-layouts: 6.2 us -> 3 us
    pallas_call x1, Pallas kernels: 104 us -> 97 us  [layer(): pl.pallas_call(layer_kernel, out_shape=(jax.ShapeDtypeStruct((TOK, HEADS_...]
    unnamed x5 -> x4, local copies, waits for them, and re-layouts: 4.86 us -> 3 us
    reshape x1 -> x0, local copies, waits for them, and re-layouts: 1.34 us -> none  [body(): norm_gain.reshape(1, D)]
where the time goes in v3:
time: 101 us
  Pallas kernels  97 us (96%)
  local copies, waits for them, and re-layouts  3 us (3%)
    pallas_call x1, Pallas kernels, layer(): pl.pallas_call(layer_kernel, out_shape=(jax.ShapeDtypeStruct((TOK, HEADS_...  97 us
    unnamed x4, local copies, waits for them, and re-layouts  3 us

profile of v3, /device:TPU:1, one launch (start us, length us, event | category | flops | bytes accessed | tf_op | source)
XLA Modules:
  0.0 100.7 jit_solution(884807227497630371)
XLA Ops:
  0.6 97.0 %shard_map.158 = (bf16[128,8,512]{2,1,0:T(8,128)(2,1)}, bf16[16,7168]{1,0:T(8,128)(2,1)}) custom-call(s32[1,16]{1,0:T(1,128)} %pages.1, s32[16]{0:T(128)} %lengths.1, bf16[576,128]{1,0:T(8,128)(2,1)} %bitcast.9, bf16[16,8,576]{2,1,0:T(8,128)(2,1)} %dec_q.1, bf16[16,576]{1,0:T(8,128)(2,1)} %dec_kv.1, bf16[16,7168]{1,0:T(8,128)(2,1)} %x_dec_in.1, ...), custom_call_target="tpu_custom_call" | custom-call | tf_op jit(solution)/shard_map/pallas_call | solution.py:583
  97.7 0.0 copy-start
  97.7 2.3 %copy.19 = bf16[128,8,512]{2,1,0:T(8,128)(2,1)} copy(bf16[128,8,512]{2,1,0:T(8,128)(2,1)} %get-tuple-element.4) | data formatting | bytes 2097152
  100.0 0.0 copy-done
  100.0 0.7 copy.20
Async XLA Ops:
  97.7 2.3 %copy-start = (bf16[16,7168]{1,0:T(8,128)(2,1)S(1)}, bf16[16,7168]{1,0:T(8,128)(2,1)}, u32[]{:S(2)}) copy-start(bf16[16,7168]{1,0:T(8,128)(2,1)} %get-tuple-element.5) | copy-start | bytes 688132

commit v4 on v3

--- a/solution.py
+++ b/solution.py
@@ -600,6 +600,27 @@
     )(*args)
 
 
+def hand_out_kernel(pref_in, out_in, pref, out, sem):
+    copies = [
+        pltpu.make_async_copy(pref_in, pref, sem.at[0]),
+        pltpu.make_async_copy(out_in, out, sem.at[1]),
+    ]
+    for made in copies:
+        made.start()
+    for made in copies:
+        made.wait()
+
+
+def hand_out(pref, out):
+    return pl.pallas_call(
+        hand_out_kernel,
+        out_shape=tuple(jax.ShapeDtypeStruct(x.shape, x.dtype) for x in (pref, out)),
+        in_specs=[pl.BlockSpec(memory_space=VMEM)] * 2,
+        out_specs=[pl.BlockSpec(memory_space=ANY)] * 2,
+        scratch_shapes=[pltpu.SemaphoreType.DMA((2,))],
+    )(pref, out)
+
+
 def body(
     q_pref,
     kv_pref,
@@ -634,7 +655,7 @@
         w_up,
         w_down,
     )
-    return (pref, decode_out)
+    return hand_out(pref, decode_out)
 
 
 def solution(mesh):

time: 101 us -> 100 us (0.990)
  local copies, waits for them, and re-layouts: 3 us -> 0 us
  Pallas kernels: 97 us -> 99.3 us
    unnamed x4 -> x0, local copies, waits for them, and re-layouts: 3 us -> none
    pallas_call x0 -> x1, Pallas kernels: none -> 2.3 us  [hand_out(): pl.pallas_call(hand_out_kernel, out_shape=tuple((jax.ShapeDtypeStruct(x.s...]
where the time goes in v4:
time: 100 us
  Pallas kernels  99.3 us (99%)
    pallas_call x1, Pallas kernels, layer(): pl.pallas_call(layer_kernel, out_shape=(jax.ShapeDtypeStruct((TOK, HEADS_...  97 us
    pallas_call x1, Pallas kernels, hand_out(): pl.pallas_call(hand_out_kernel, out_shape=tuple((jax.ShapeDtypeStruct(x.s...  2.3 us

profile of v4, /device:TPU:1, one launch (start us, length us, event | category | flops | bytes accessed | tf_op | source)
XLA Modules:
  0.0 100.1 jit_solution(10916187002831741755)
XLA Ops:
  0.6 97.0 %shard_map.158 = (bf16[128,8,512]{2,1,0:T(8,128)(2,1)}, bf16[16,7168]{1,0:T(8,128)(2,1)}) custom-call(s32[1,16]{1,0:T(1,128)} %pages.1, s32[16]{0:T(128)} %lengths.1, bf16[576,128]{1,0:T(8,128)(2,1)} %bitcast.9, bf16[16,8,576]{2,1,0:T(8,128)(2,1)} %dec_q.1, bf16[16,576]{1,0:T(8,128)(2,1)} %dec_kv.1, bf16[16,7168]{1,0:T(8,128)(2,1)} %x_dec_in.1, ...), custom_call_target="tpu_custom_call" | custom-call | tf_op jit(solution)/shard_map/pallas_call | solution.py:583
  97.7 2.3 %shard_map.159 = (bf16[128,8,512]{2,1,0:T(8,128)(2,1)}, bf16[16,7168]{1,0:T(8,128)(2,1)}) custom-call(bf16[128,8,512]{2,1,0:T(8,128)(2,1)} %get-tuple-element.4.pref_in, bf16[16,7168]{1,0:T(8,128)(2,1)} %get-tuple-element.5.out_in), custom_call_target="tpu_custom_call" | custom-call | tf_op jit(solution)/shard_map/pallas_call | solution.py:615
